TPU v7x, 32 devices: a whole 2x2x4 slice. The times are simulated.
32 devices in a mesh: groups: 2 (over y), pulse: 4 (over z), range: 2 (over x), sub: 2 (over core).
Axes of the slice: x: 2, y: 2, z: 4, core: 2. Of those that a mesh axis runs over, the one named last changes fastest.
Arguments:
- raw_echo: bfloat16 [2, 128, 16384], P(None, ('groups', 'pulse', 'sub'), 'range'), parts along dimension 1, may hold values from -6 to 6
- range_taps: bfloat16 [32, 512, 128], P('pulse'), may hold values from -0.25 to 0.25
- azim_taps: bfloat16 [128, 2048], P(('groups', 'pulse', 'sub')), parts along dimension 0, may hold values from -1 to 1
- tile_col: int32 [128, 1], P(('groups', 'pulse', 'sub')), parts along dimension 0, may hold values from 0 to 1; in each aligned block of 4 rows (0 to 3, 4 to 7, ...) at most 2 rows name the same one
Outputs:
- image: float32 [2, 8192, 4096], P(None, ('groups', 'pulse', 'range', 'sub')), parts along dimension 1
There are 2 independent parts, one for each index of `groups`. A program takes and returns all parts, laid end to end along the dimension named above; an argument that names none is the same for every part. Nothing has to cross between parts.
Inputs may be any that keep to these rules, and one draw needn't show every extreme that they name: `tile_col`: in each aligned block of 4 pulses no tile column is named by more than 2 pulses.
All inputs are finite; a program needn't handle non-finite values.
Results may differ from a plain program's by a relative error of at most 0.008.
Values may be sent and summed in bfloat16 or wider, within the bound.
A program may use at most 64 MiB of HBM per device.

v0:
```python
import math

import jax
import jax.numpy as jnp
from jax import lax
from jax.sharding import PartitionSpec as P

CAP = 2


def swapped(block, axis, bit):
    count = lax.axis_size(axis)
    route = []
    for low in range(count):
        high = low | 1 << bit
        if high != low and high < count:
            route += [(low, high), (high, low)]
    return lax.ppermute(block, axis, route)


def as_sent(value):
    return jax.tree.map(lambda a: a.astype(jnp.bfloat16) if a.dtype == jnp.float32 else a, value)


def tables(points, direction):
    indices = jnp.arange(points, dtype=jnp.int32)
    phases = indices[:, None] * indices[None, :] % points
    angles = phases.astype(jnp.float32) * (2.0 * math.pi / points)
    return (jnp.cos(angles), direction * jnp.sin(angles))


def spectral(real_part, imag_part, direction):
    length = real_part.shape[-1]
    outer_len = 1 << (length.bit_length() - 1) // 2
    inner_len = length // outer_len
    leading = real_part.shape[:-1]
    real_part = real_part.reshape(leading + (outer_len, inner_len))
    imag_part = imag_part.reshape(leading + (outer_len, inner_len))
    highest = lax.Precision.HIGHEST
    cos_outer, sin_outer = tables(outer_len, direction)
    mixed_real = jnp.einsum(
        "...nm,nk->...km", real_part, cos_outer, precision=highest
    ) - jnp.einsum("...nm,nk->...km", imag_part, sin_outer, precision=highest)
    mixed_imag = jnp.einsum(
        "...nm,nk->...km", real_part, sin_outer, precision=highest
    ) + jnp.einsum("...nm,nk->...km", imag_part, cos_outer, precision=highest)
    outer_index = jnp.arange(outer_len, dtype=jnp.int32)[:, None]
    inner_index = jnp.arange(inner_len, dtype=jnp.int32)[None, :]
    twists = (outer_index * inner_index % length).astype(jnp.float32) * (2.0 * math.pi / length)
    twist_cos = jnp.cos(twists)
    twist_sin = direction * jnp.sin(twists)
    turned_real = mixed_real * twist_cos - mixed_imag * twist_sin
    turned_imag = mixed_real * twist_sin + mixed_imag * twist_cos
    cos_inner, sin_inner = tables(inner_len, direction)
    final_real = jnp.einsum(
        "...km,mj->...jk", turned_real, cos_inner, precision=highest
    ) - jnp.einsum("...km,mj->...jk", turned_imag, sin_inner, precision=highest)
    final_imag = jnp.einsum(
        "...km,mj->...jk", turned_real, sin_inner, precision=highest
    ) + jnp.einsum("...km,mj->...jk", turned_imag, cos_inner, precision=highest)
    norm_scale = 1.0 / math.sqrt(length)
    return (
        (final_real * norm_scale).reshape(leading + (length,)),
        (final_imag * norm_scale).reshape(leading + (length,)),
    )


def body(raw_echo, range_taps, azim_taps, tile_col):
    n_range = lax.axis_size("range")
    n_pulse = lax.axis_size("pulse")
    my_range = lax.axis_index("range")
    my_sub = lax.axis_index("sub")
    shard_pulses = raw_echo.shape[1]
    shard_samples = raw_echo.shape[2]
    per_device = shard_pulses // n_range
    grouped = raw_echo.reshape(2, n_range, per_device, shard_samples)
    pieces = lax.all_to_all(grouped, "range", split_axis=1, concat_axis=3, tiled=True)
    real_out, imag_out = spectral(
        pieces[0].astype(jnp.float32), pieces[1].astype(jnp.float32), -1.0
    )
    spectrum = jnp.stack([real_out, imag_out]).astype(jnp.bfloat16)
    spectrum = spectrum.reshape(2, per_device, shard_samples * n_range)
    band_bins = spectrum.shape[2] // n_pulse
    first_pulse = my_range * per_device
    cols_here = lax.dynamic_slice_in_dim(tile_col[:, 0], first_pulse, per_device)
    taps_here = lax.dynamic_slice_in_dim(azim_taps, first_pulse, per_device, 0)
    position = jnp.arange(per_device, dtype=jnp.int32)
    earlier = position[None, :] < position[:, None]
    same_tile = cols_here[:, None] == cols_here[None, :]
    slot_rank = jnp.sum(jnp.where(earlier & same_tile, 1, 0), axis=1)
    tile_ids = jnp.arange(n_range, dtype=jnp.int32)
    slot_ids = jnp.arange(CAP, dtype=jnp.int32)
    placing = (
        (cols_here[None, None, :] == tile_ids[:, None, None])
        & (slot_rank[None, None, :] == slot_ids[None, :, None])
    ).astype(jnp.bfloat16)
    banded = spectrum.reshape(2, per_device, n_pulse, band_bins)
    send_lines = jnp.einsum(
        "tcq,xqpb->ptcxb", placing, banded, preferred_element_type=jnp.float32
    ).astype(jnp.bfloat16)
    send_taps = jnp.einsum(
        "tcq,qw->tcw", placing, taps_here, preferred_element_type=jnp.float32
    ).astype(jnp.bfloat16)
    tile_width = send_taps.shape[2]
    send_taps = jnp.broadcast_to(send_taps[None], (n_pulse, n_range, CAP, tile_width))
    block_count, block_bins, block_rows = range_taps.shape
    flat_lines = send_lines.reshape(n_pulse * n_range, CAP, 2, band_bins)
    flat_taps = send_taps.reshape(n_pulse * n_range, CAP, tile_width)
    line_block = lax.all_to_all(
        flat_lines, ("pulse", "range"), split_axis=0, concat_axis=0, tiled=True
    )
    tap_block = lax.all_to_all(
        flat_taps, ("pulse", "range"), split_axis=0, concat_axis=0, tiled=True
    )
    blocked = line_block.reshape(line_block.shape[:3] + (block_count, block_bins))
    resampled = jnp.einsum(
        "skxbr,brj->skxbj", blocked, range_taps, preferred_element_type=jnp.float32
    )
    ky_rows = resampled.reshape(line_block.shape[:3] + (block_count * block_rows,)).astype(
        jnp.bfloat16
    )
    band_rows = ky_rows.shape[3]
    slot_total = ky_rows.shape[0] * ky_rows.shape[1]
    slot_lines = ky_rows.reshape(slot_total, 2, band_rows)
    slot_taps = tap_block.reshape(slot_total, tile_width)
    half_width = tile_width // 2
    other_lines, other_taps = swapped((slot_lines, slot_taps), "sub", 0)
    column_start = my_sub * half_width
    my_taps = lax.dynamic_slice_in_dim(slot_taps, column_start, half_width, 1)
    their_taps = lax.dynamic_slice_in_dim(other_taps, column_start, half_width, 1)
    own_part = jnp.einsum("mi,mxj->xij", my_taps, slot_lines, preferred_element_type=jnp.float32)
    far_part = jnp.einsum(
        "mi,mxj->xij", their_taps, other_lines, preferred_element_type=jnp.float32
    )
    own_round = lax.optimization_barrier(own_part.astype(jnp.bfloat16))
    far_round = lax.optimization_barrier(far_part.astype(jnp.bfloat16))
    kspace = own_round.astype(jnp.float32) + far_round.astype(jnp.float32)
    pieces_each = half_width // n_pulse
    shaped = kspace.reshape(2, n_pulse, pieces_each, band_rows)
    pieces = lax.all_to_all(
        shaped.astype(jnp.bfloat16), "pulse", split_axis=1, concat_axis=3, tiled=True
    ).astype(shaped.dtype)
    real_out, imag_out = spectral(pieces[0], pieces[1], 1.0)
    columns_done = jnp.stack([real_out, imag_out])
    columns_done = columns_done.reshape(2, pieces_each, band_rows * n_pulse)
    moved = lax.all_to_all(
        lax.all_to_all(as_sent(columns_done), "pulse", split_axis=2, concat_axis=1, tiled=True),
        ("range", "sub"),
        split_axis=2,
        concat_axis=1,
        tiled=True,
    ).astype(columns_done.dtype)
    flipped = jnp.swapaxes(moved, 1, 2)
    real_out, imag_out = spectral(flipped[0], flipped[1], 1.0)
    return jnp.stack([real_out, imag_out])


def solution(mesh):
    placed = (
        P(None, ("groups", "pulse", "sub"), "range"),
        P("pulse", None, None),
        P(("groups", "pulse", "sub"), None),
        P(("groups", "pulse", "sub"), None),
    )
    return jax.shard_map(
        body,
        mesh=mesh,
        in_specs=placed,
        out_specs=P(None, ("groups", "pulse", "range", "sub"), None),
        check_vma=False,
    )
```

profile of v0, /device:TPU:0, one launch (start us, length us, event | category | flops | bytes accessed | tf_op | source)
XLA Modules:
  0.0 452.3 jit_solution(6309015719633737124)
XLA Ops:
  2.2 4.2 all-to-all-start
  13.0 5.1 %all-to-all-start.2 = ((bf16[8,2,2048]{2,1,0:T(2,128)(2,1)}), bf16[8,2,2048]{2,1,0:T(2,128)(2,1)S(1)}, u32[]{:S(2)}, u32[]{:S(2)}) async-start(bf16[8,2,2048]{2,1,0:T(2,128)(2,1)} %bitcast.30), calls=%async_computation.2 | async-start | bytes 131072 | tf_op jit(solution)/shard_map/all_to_all | solution.py:112
  25.1 6.3 %all-to-all-start.1 = ((bf16[8,2,2,4096]{3,2,1,0:T(2,128)(2,1)}), bf16[8,2,2,4096]{3,2,1,0:T(2,128)(2,1)S(1)}, u32[]{:S(2)}, u32[]{:S(2)}) async-start(bf16[8,2,2,4096]{3,2,1,0:T(2,128)(2,1)} %copy.134), calls=%async_computation.1 | async-start | bytes 524288 | tf_op jit(solution)/shard_map/all_to_all | solution.py:109
  31.6 8.1 %all-to-all-done.1 = bf16[8,2,2,4096]{3,2,1,0:T(2,128)(2,1)S(1)} async-done(((bf16[8,2,2,4096]{3,2,1,0:T(2,128)(2,1)}), bf16[8,2,2,4096]{3,2,1,0:T(2,128)(2,1)S(1)}, u32[]{:S(2)}, u32[]{:S(2)}) %all-to-all-start.1) | async-done | bytes 262176 | tf_op jit(solution)/shard_map/all_to_all | solution.py:109
  47.5 5.4 %all-to-all-start.3 = ((bf16[2,4,256,1024]{2,3,0,1:T(8,128)(2,1)}), bf16[2,4,256,1024]{2,3,0,1:T(8,128)(2,1)}, u32[]{:S(2)}, u32[]{:S(2)}) async-start(bf16[2,4,256,1024]{2,3,0,1:T(8,128)(2,1)} %bitcast.216), calls=%async_computation.3 | async-start | bytes 8388608 | tf_op jit(solution)/shard_map/all_to_all | solution.py:140
  53.0 93.5 %all-to-all-done.3 = bf16[2,4,256,1024]{2,3,0,1:T(8,128)(2,1)} async-done(((bf16[2,4,256,1024]{2,3,0,1:T(8,128)(2,1)}), bf16[2,4,256,1024]{2,3,0,1:T(8,128)(2,1)}, u32[]{:S(2)}, u32[]{:S(2)}) %all-to-all-start.3) | async-done | bytes 4194336 | tf_op jit(solution)/shard_map/all_to_all | solution.py:140
  157.7 4.7 %fusion.1 = (f32[256,64,64]{0,1,2:T(8,128)S(1)}, f32[256,64,64]{0,1,2:T(8,128)S(1)}) fusion(f32[64,256,64]{1,0,2:T(8,128)S(1)} %convolution_add_fusion.1, f32[64,64]{0,1:T(8,128)S(1)} %get-tuple-element.17, f32[64,64]{0,1:T(8,128)S(1)} %get-tuple-element.18, f32[64,256,64]{1,0,2:T(8,128)S(1)} %fusion.40, bf16[256,64,64]{0,2,1:T(8,128)(2,1)S(1)} %bitcast.210), kind=kOutput, calls=%fused_computation.8 | convolution fusion | flops 812703744 | bytes 18907136 | tf_op jit(solution)/shard_map/...nm,nk->...km/dot_general | solution.py:43
  162.4 6.3 %fusion.12 = f32[64,256,64]{1,0,2:T(8,128)S(1)} fusion(f32[256,64,64]{0,1,2:T(8,128)S(1)} %get-tuple-element.8), kind=kOutput, calls=%fused_computation.30 | convolution fusion | flops 805363712 | bytes 8388608 | tf_op jit(solution)/shard_map/...km,mj->...jk/dot_general | solution.py:60
  168.7 6.5 %fusion.14 = f32[64,256,64]{1,0,2:T(8,128)S(1)} fusion(f32[256,64,64]{0,1,2:T(8,128)S(1)} %get-tuple-element.8), kind=kOutput, calls=%fused_computation.32 | convolution fusion | flops 805363712 | bytes 8388608 | tf_op jit(solution)/shard_map/...km,mj->...jk/dot_general | solution.py:57
  175.2 6.0 %fusion.25 = bf16[1,256,64,64]{1,2,3,0:T(8,128)(2,1)S(1)} fusion(f32[64,256,64]{1,0,2:T(8,128)S(1)} %fusion.12, f32[256,64,64]{0,1,2:T(8,128)S(1)} %get-tuple-element.7), kind=kOutput, calls=%fused_computation.44 | convolution fusion | flops 808509440 | bytes 10485760 | tf_op jit(solution)/shard_map/...km,mj->...jk/dot_general | solution.py:58
  182.4 5.9 %fusion.24 = bf16[1,256,64,64]{1,2,3,0:T(8,128)(2,1)S(1)} fusion(f32[64,256,64]{1,0,2:T(8,128)S(1)} %fusion.14, f32[256,64,64]{0,1,2:T(8,128)S(1)} %get-tuple-element.7), kind=kOutput, calls=%fused_computation.43 | convolution fusion | flops 808509440 | bytes 10485760 | tf_op jit(solution)/shard_map/...km,mj->...jk/dot_general | solution.py:55
  189.9 25.5 %copy.150 = bf16[2,256,4096]{1,0,2:T(2,128)(2,1)S(1)} copy(bf16[2,256,4096]{1,2,0:T(8,128)(2,1)S(1)} %maximum_bitcast_fusion) | data formatting | bytes 8388608 | tf_op jit(solution)/shard_map/convert_element_type | solution.py:22
  215.3 95.9 %all_to_all.76 = bf16[2,256,4096]{1,0,2:T(2,128)(2,1)S(1)} all-to-all(bf16[2,256,4096]{1,0,2:T(2,128)(2,1)S(1)} %copy.150), channel_id=1, replica_groups=mesh['groups'=2,'pulse'=4,'range'=2,'sub'=2] {'pulse'}, dimensions={2} | all-to-all | bytes 8388608 | tf_op jit(solution)/shard_map/all_to_all | solution.py:147
  313.8 6.3 %copy.152 = bf16[2,4,256,1024]{3,2,1,0:T(8,128)(2,1)} copy(bf16[2,4,256,1024]{2,3,1,0:T(8,128)(2,1)} %bitcast.219) | data formatting | bytes 8388608 | tf_op jit(solution)/shard_map/all_to_all | solution.py:147
  320.0 11.3 %copy.153 = bf16[2,1024,1024]{1,0,2:T(2,128)(2,1)} copy(bf16[2,1024,1024]{2,1,0:T(8,128)(2,1)} %bitcast.220) | data formatting | bytes 8388608 | tf_op jit(solution)/shard_map/all_to_all | solution.py:147
  331.3 51.9 %all_to_all.77 = bf16[2,1024,1024]{1,0,2:T(2,128)(2,1)S(1)} all-to-all(bf16[2,1024,1024]{1,0,2:T(2,128)(2,1)} %copy.153), channel_id=1, replica_groups=mesh['groups'=2,'pulse'=4,'range'=2,'sub'=2] {'range','sub'}, dimensions={2} | all-to-all | bytes 8388608 | tf_op jit(solution)/shard_map/all_to_all | solution.py:146
  386.5 6.4 %copy.155 = bf16[2,4,1024,256]{3,2,1,0:T(8,128)(2,1)} copy(bf16[2,4,1024,256]{2,3,1,0:T(8,128)(2,1)} %bitcast.221) | data formatting | bytes 8388608 | tf_op jit(solution)/shard_map/all_to_all | solution.py:146
  403.9 4.7 %subtract_bitcast_fusion = (f32[256,64,64]{0,1,2:T(8,128)S(1)}, f32[256,64,64]{0,1,2:T(8,128)S(1)}) fusion(f32[64,256,64]{1,0,2:T(8,128)S(1)} %convolution_add_fusion, f32[64,64]{0,1:T(8,128)S(1)} %get-tuple-element.17, f32[64,64]{0,1:T(8,128)S(1)} %get-tuple-element.18, f32[64,256,64]{1,0,2:T(8,128)S(1)} %fusion.34, bf16[256,64,64]{0,2,1:T(8,128)(2,1)S(1)} %bitcast.208), kind=kOutput, calls=%fused_computation.17 | convolution fusion | flops 812703744 | bytes 18907136 | tf_op jit(solution)/shard_map/...nm,nk->...km/dot_general | solution.py:43
  408.6 6.0 %fusion.4 = f32[64,256,64]{1,0,2:T(8,128)S(1)} fusion(f32[256,64,64]{0,1,2:T(8,128)S(1)} %get-tuple-element.6), kind=kOutput, calls=%fused_computation.22 | convolution fusion | flops 805363712 | bytes 8388608 | tf_op jit(solution)/shard_map/...km,mj->...jk/dot_general | solution.py:60
  414.7 6.7 %fusion.6 = f32[64,256,64]{1,0,2:T(8,128)S(1)} fusion(f32[256,64,64]{0,1,2:T(8,128)S(1)} %get-tuple-element.6), kind=kOutput, calls=%fused_computation.24 | convolution fusion | flops 805363712 | bytes 8388608 | tf_op jit(solution)/shard_map/...km,mj->...jk/dot_general | solution.py:57
  421.4 6.4 %multiply_bitcast_fusion.1 = f32[256,64,64]{0,1,2:T(8,128)S(1)} fusion(f32[64,256,64]{1,0,2:T(8,128)S(1)} %fusion.6, f32[256,64,64]{0,1,2:T(8,128)S(1)} %get-tuple-element.5), kind=kOutput, calls=%fused_computation.15 | convolution fusion | flops 807460864 | bytes 12582912 | tf_op jit(solution)/shard_map/...km,mj->...jk/dot_general | solution.py:55
  427.8 6.7 %multiply_bitcast_fusion = f32[256,64,64]{0,1,2:T(8,128)S(1)} fusion(f32[64,256,64]{1,0,2:T(8,128)S(1)} %fusion.4, f32[256,64,64]{0,1,2:T(8,128)S(1)} %get-tuple-element.5), kind=kOutput, calls=%fused_computation.14 | convolution fusion | flops 807460864 | bytes 12582912 | tf_op jit(solution)/shard_map/...km,mj->...jk/dot_general | solution.py:58
  439.4 3.8 pad_maximum_fusion
  443.1 9.0 %copy.166 = f32[2,256,4096]{2,1,0:T(8,128)} copy(f32[2,256,4096]{1,2,0:T(8,128)} %pad_maximum_fusion) | data formatting | bytes 16777216 | tf_op jit(solution)/shard_map/stack | solution.py:155
  (66 shorter events, 59.4 us)
Async XLA Ops:
  0.0 39.8 %copy-start = (bf16[8,512,128]{2,1,0:T(8,128)(2,1)S(1)}, bf16[8,512,128]{2,1,0:T(8,128)(2,1)}, u32[]{:S(2)}) copy-start(bf16[8,512,128]{2,1,0:T(8,128)(2,1)} %param.5) | copy-start | bytes 3145732
  2.2 10.1 %all-to-all-start = ((bf16[2,2,4,8192]{3,2,0,1:T(4,128)(2,1)}), bf16[2,2,4,8192]{3,2,0,1:T(4,128)(2,1)S(1)}, u32[]{:S(2)}, u32[]{:S(2)}) async-start(bf16[2,2,4,8192]{3,2,0,1:T(4,128)(2,1)} %copy.127), calls=%async_computation | async-start | bytes 524288 | tf_op jit(solution)/shard_map/all_to_all | solution.py:77
  13.0 12.2 %all-to-all-start.2 = ((bf16[8,2,2048]{2,1,0:T(2,128)(2,1)}), bf16[8,2,2048]{2,1,0:T(2,128)(2,1)S(1)}, u32[]{:S(2)}, u32[]{:S(2)}) async-start(bf16[8,2,2048]{2,1,0:T(2,128)(2,1)} %bitcast.30), calls=%async_computation.2 | async-start | bytes 131072 | tf_op jit(solution)/shard_map/all_to_all | solution.py:112
  25.1 14.5 %all-to-all-start.1 = ((bf16[8,2,2,4096]{3,2,1,0:T(2,128)(2,1)}), bf16[8,2,2,4096]{3,2,1,0:T(2,128)(2,1)S(1)}, u32[]{:S(2)}, u32[]{:S(2)}) async-start(bf16[8,2,2,4096]{3,2,1,0:T(2,128)(2,1)} %copy.134), calls=%async_computation.1 | async-start | bytes 524288 | tf_op jit(solution)/shard_map/all_to_all | solution.py:109
  31.5 10.1 %collective-permute-start.1 = (bf16[16,2048]{1,0:T(8,128)(2,1)S(1)}, bf16[16,2048]{1,0:T(8,128)(2,1)S(1)}, u32[]{:S(2)}, u32[]{:S(2)}) collective-permute-start(bf16[16,2048]{1,0:T(8,128)(2,1)S(1)} %reshape.306), channel_id=1, source_target_pairs={{0,1},{1,0},{2,3},{3,2},{4,5},{5,4},{6,7},{7,6},{8,9},{9,8},{10,11... | collective-permute-start | bytes 196616 | tf_op jit(solution)/shard_map/ppermute | solution.py:18
  40.3 1.4 collective-permute-start
  47.5 99.0 %all-to-all-start.3 = ((bf16[2,4,256,1024]{2,3,0,1:T(8,128)(2,1)}), bf16[2,4,256,1024]{2,3,0,1:T(8,128)(2,1)}, u32[]{:S(2)}, u32[]{:S(2)}) async-start(bf16[2,4,256,1024]{2,3,0,1:T(8,128)(2,1)} %bitcast.216), calls=%async_computation.3 | async-start | bytes 8388608 | tf_op jit(solution)/shard_map/all_to_all | solution.py:140
  443.1 9.0 %copy-start.1 = (bf16[8,512,128]{2,1,0:T(8,128)(2,1)S(1)}, bf16[8,512,128]{2,1,0:T(8,128)(2,1)}, u32[]{:S(2)}) copy-start(bf16[8,512,128]{2,1,0:T(8,128)(2,1)} %param.5) | copy-start | bytes 3145732
where the time goes:
time: 459 us; the launch traced here: 452 us
  blocking collectives  148 us (32%)
  waiting for transfers between devices  105 us (23%)
  matrix products  85.8 us (19%)
  local copies, waits for them, and re-layouts  84.9 us (18%)
  starting transfers between devices  21.2 us (5%)
  other arithmetic  7.26 us (2%)
    all_to_all x1, blocking collectives, body(): lax.all_to_all(as_sent(columns_done), 'pulse', split_axis=2, concat_axis=...  95.9 us
    all_to_all x1, waiting for transfers between devices, body(): lax.all_to_all(shaped.astype(jnp.bfloat16), 'pulse', split_axis=1, concat...  93.5 us
    all_to_all x1, blocking collectives, body(): lax.all_to_all(lax.all_to_all(as_sent(columns_done), 'pulse', split_axis=...  51.9 us
    convert_element_type x1, local copies, waits for them, and re-layouts, as_sent(): a.astype(jnp.bfloat16)  25.5 us
    all_to_all x3, local copies, waits for them, and re-layouts, body(): lax.all_to_all(as_sent(columns_done), 'pulse', split_axis=2, concat_axis=...  20.1 us
    dot_general x3, matrix products, spectral(): jnp.einsum('...km,mj->...jk', turned_imag, sin_inner, precision=highest)  13.9 us
    dot_general x3, matrix products, spectral(): jnp.einsum('...km,mj->...jk', turned_real, sin_inner, precision=highest)  13.4 us
    dot_general x3, matrix products, spectral(): jnp.einsum('...km,mj->...jk', turned_imag, cos_inner, precision=highest)  13 us
  transfers between devices with their start and end apart: 6, of which 3 were waited for; matrix products, arithmetic and copies ran while one was open for 3% of the time, Pallas kernels for 0%

commit v1 on v0

--- a/solution.py
+++ b/solution.py
@@ -1,8 +1,13 @@
+import functools
 import math
 
 import jax
 import jax.numpy as jnp
+import ml_dtypes
+import numpy as np
 from jax import lax
+from jax.experimental import pallas as pl
+from jax.experimental.pallas import tpu as pltpu
 from jax.sharding import PartitionSpec as P
 
 CAP = 2
@@ -65,7 +70,7 @@
     )
 
 
-def body(raw_echo, range_taps, azim_taps, tile_col):
+def general_body(raw_echo, range_taps, azim_taps, tile_col):
     n_range = lax.axis_size("range")
     n_pulse = lax.axis_size("pulse")
     my_range = lax.axis_index("range")
@@ -155,6 +160,355 @@
     return jnp.stack([real_out, imag_out])
 
 
+LANES = 128
+BF16 = jnp.bfloat16
+F32 = jnp.float32
+MESH = pl.DeviceIdType.MESH
+
+
+def split_bf16(table):
+    high = table.astype(ml_dtypes.bfloat16)
+    low = (table - high.astype(np.float64)).astype(ml_dtypes.bfloat16)
+    return np.stack([high, low])
+
+
+def turn(fraction):
+    return np.exp(2j * np.pi * (fraction % 1.0))
+
+
+def pulse_tables(samples, n_range):
+    rows = samples // LANES
+    k = np.arange(LANES)
+    first = turn(-np.outer(k, np.arange(rows)) / rows) / math.sqrt(samples)
+    parts = first.reshape(LANES, n_range, rows // n_range)
+    real = np.stack([parts.real, -parts.imag], axis=2).reshape(LANES, 2 * rows)
+    imag = np.stack([parts.imag, parts.real], axis=2).reshape(LANES, 2 * rows)
+    left = split_bf16(np.concatenate([real, imag]))
+    second = turn(-np.outer(k, k) / LANES)
+    right = split_bf16(np.block([[second.real, -second.imag], [second.imag, second.real]]))
+    twist = turn(-np.outer(k, k) / samples)
+    return left, right, np.stack([twist.real, twist.imag]).astype(np.float32)
+
+
+def column_tables(grid, n_pulse, rows, devices):
+    band = grid // n_pulse
+    u = np.arange(grid).reshape(n_pulse, 1, band)
+    angle = turn(u * np.arange(rows)[None, :, None] / grid) / math.sqrt(grid)
+    table = np.concatenate([angle.real, angle.imag], axis=2).astype(ml_dtypes.bfloat16)
+    shift = turn(np.outer(np.arange(devices) * rows, np.arange(LANES)) / grid)
+    return table, np.stack([shift.real, shift.imag]).astype(np.float32)[:, :, None, :]
+
+
+def row_table(grid, width):
+    upper = grid // LANES
+    half = upper // 2
+    f = np.arange(half)[:, None, None, None, None]
+    e = np.arange(2)[None, :, None, None, None]
+    i1 = np.arange(width // upper)[None, None, :, None, None]
+    parity = np.arange(2)[None, None, None, :, None]
+    x1 = np.arange(LANES)[None, None, None, None, :]
+    taps = upper * i1 + half * e + f
+    angle = turn(taps * x1 / grid + (half * e + f) * parity / upper) / math.sqrt(grid)
+    both = np.stack([angle.real, angle.imag], axis=4)
+    return both.reshape(half, 2 * (width // upper), 4 * LANES).astype(ml_dtypes.bfloat16)
+
+
+def plane_transform(real, imag):
+    count = len(real)
+    if count == 1:
+        return real, imag
+    even_r, even_i = plane_transform(real[0::2], imag[0::2])
+    odd_r, odd_i = plane_transform(real[1::2], imag[1::2])
+    low_r, low_i, high_r, high_i = [], [], [], []
+    for k in range(count // 2):
+        a, b = odd_r[k], odd_i[k]
+        if k == 0:
+            tr, ti = a, b
+        elif 4 * k == count:
+            tr, ti = -b, a
+        else:
+            c = math.cos(2.0 * math.pi * k / count)
+            s = math.sin(2.0 * math.pi * k / count)
+            tr, ti = a * c - b * s, a * s + b * c
+        low_r.append(even_r[k] + tr)
+        low_i.append(even_i[k] + ti)
+        high_r.append(even_r[k] - tr)
+        high_i.append(even_i[k] - ti)
+    return low_r + high_r, low_i + high_i
+
+
+def matmul(a, b):
+    return jnp.dot(a, b, preferred_element_type=F32)
+
+
+def matmul_nt(a, b):
+    return lax.dot_general(a, b, (((1,), (1,)), ((), ())), preferred_element_type=F32)
+
+
+def form_kernel(
+    sizes,
+    raw_ref, az_ref, left_ref, right_ref, twist_ref, shift_ref, taps_ref, rowtab_ref, coltab_ref,
+    lhs_ref, rhs_ref,
+    x_buf, az_buf, sp_out, sp_in, sp_f32, planes, turned, col_buf, part_out, part_in, sums,
+    local_sem, x_send, x_recv, az_send, az_recv, sp_send, sp_recv, part_send, part_recv,
+):
+    n_pulse, n_range, n_sub = sizes
+    devices = n_pulse * n_range * n_sub
+    z, x, s = lax.axis_index("pulse"), lax.axis_index("range"), lax.axis_index("sub")
+    me = (z * n_range + x) * n_sub + s
+    shards = n_pulse * n_sub
+    shard = z * n_sub + s
+    pulses = x_buf.shape[2]
+    blocks = taps_ref.shape[0]
+    band_rows = sp_in.shape[3]
+
+    def whole_id(index):
+        rest = index // n_sub
+        return {"pulse": rest // n_range, "range": rest % n_range, "sub": index % n_sub}
+
+    table_copy = pltpu.make_async_copy(coltab_ref.at[z], col_buf, local_sem.at[0])
+    table_copy.start()
+    own_raw = pltpu.make_async_copy(raw_ref.at[:, pl.ds(x * pulses, pulses)], x_buf.at[x], local_sem.at[1])
+    own_raw.start()
+    own_az = pltpu.make_async_copy(az_ref, az_buf.at[shard], local_sem.at[2])
+    own_az.start()
+
+    barrier = pltpu.get_barrier_semaphore()
+    for r in range(1, devices):
+        pl.semaphore_signal(barrier, inc=1, device_id=whole_id((me + r) % devices), device_id_type=MESH)
+    pl.semaphore_wait(barrier, devices - 1)
+
+    raw_copies = []
+    for r in range(1, n_range):
+        other = (x + r) % n_range
+        copy = pltpu.make_async_remote_copy(
+            raw_ref.at[:, pl.ds(other * pulses, pulses)], x_buf.at[x], x_send.at[r], x_recv.at[r],
+            device_id={"pulse": z, "range": other, "sub": s}, device_id_type=MESH)
+        copy.start()
+        raw_copies.append(copy)
+    az_copies = []
+    for r in range(1, shards):
+        other = (shard + r) % shards
+        copy = pltpu.make_async_remote_copy(
+            az_ref, az_buf.at[shard], az_send.at[r], az_recv.at[r],
+            device_id={"pulse": other // n_sub, "range": x, "sub": other % n_sub}, device_id_type=MESH)
+        copy.start()
+        az_copies.append(copy)
+
+    own_raw.wait()
+    for copy in raw_copies:
+        copy.wait()
+
+    twist_r, twist_i = twist_ref[0], twist_ref[1]
+    for p in range(pulses):
+        samples = jnp.concatenate(
+            [x_buf[h, c, p] for h in range(n_range) for c in range(2)], axis=0)
+        mixed = matmul(left_ref[0], samples) + matmul(left_ref[1], samples)
+        mr, mi = mixed[:LANES], mixed[LANES:]
+        both = jnp.concatenate([mr * twist_r - mi * twist_i, mr * twist_i + mi * twist_r], axis=1)
+        high = both.astype(BF16)
+        low = (both - high.astype(F32)).astype(BF16)
+        bins = (matmul_nt(right_ref[0], high) + matmul_nt(right_ref[1], high)
+                + matmul_nt(right_ref[0], low)).astype(BF16)
+        for c in range(2):
+            for d in range(n_pulse):
+                start = c * LANES + d * band_rows
+                sp_out[d, c, p] = bins[start:start + band_rows]
+
+    own_bins = pltpu.make_async_copy(sp_out.at[z], sp_in.at[z], local_sem.at[1])
+    own_bins.start()
+    bin_copies = []
+    for r in range(1, n_pulse):
+        other = (z + r) % n_pulse
+        copy = pltpu.make_async_remote_copy(
+            sp_out.at[other], sp_in.at[z], sp_send.at[r], sp_recv.at[r],
+            device_id={"pulse": other, "range": x, "sub": s}, device_id_type=MESH)
+        copy.start()
+        bin_copies.append(copy)
+
+    own_az.wait()
+    for copy in az_copies:
+        copy.wait()
+    residues = rowtab_ref.shape[0]
+    per_shard = az_ref.shape[0] // (residues + 2)
+    everything = [az_buf[q].astype(F32) for q in range(shards)]
+
+    def of_residue(f):
+        return jnp.concatenate([a[f * per_shard:(f + 1) * per_shard] for a in everything], axis=0)
+
+    for f in range(residues):
+        planes[f] = matmul(of_residue(f).astype(BF16), rowtab_ref[f])
+    total = shards * per_shard
+    planes[residues, :, 0:LANES] = of_residue(residues)
+    planes[residues, :, LANES:2 * LANES] = of_residue(residues + 1)
+    step_rows = 16
+
+    def row_step(i, carry):
+        rows = pl.ds(pl.multiple_of(i * step_rows, step_rows), step_rows)
+        rows_i = pl.ds(pl.multiple_of(total + i * step_rows, step_rows), step_rows)
+        pr = planes[residues, rows, 0:LANES]
+        pi = planes[residues, rows, LANES:2 * LANES]
+        for parity in range(2):
+            at = 2 * parity * LANES
+            real = [planes[f, rows, at:at + LANES] for f in range(residues)]
+            imag = [planes[f, rows, at + LANES:at + 2 * LANES] for f in range(residues)]
+            real, imag = plane_transform(real, imag)
+            for k in range(residues):
+                lane = (2 * k + parity) * LANES
+                rhs_ref[rows, lane:lane + LANES] = (real[k] * pr - imag[k] * pi).astype(BF16)
+                rhs_ref[rows_i, lane:lane + LANES] = (real[k] * pi + imag[k] * pr).astype(BF16)
+        return carry
+
+    lax.fori_loop(0, total // step_rows, row_step, 0)
+
+    own_bins.wait()
+    for copy in bin_copies:
+        copy.wait()
+    lines = n_pulse * pulses
+    for d in range(n_pulse):
+        for c in range(2):
+            for p in range(pulses):
+                at = ((c * n_pulse + d) * pulses + p) * band_rows
+                sp_f32[at:at + band_rows] = sp_in[d, c, p].astype(F32)
+    per_block = band_rows // blocks
+    band = blocks * LANES
+    shift_r, shift_i = shift_ref[0], shift_ref[1]
+    for b in range(blocks):
+        bins = jnp.concatenate(
+            [sp_f32[pl.ds(b * per_block + q, 2 * lines, stride=band_rows), :] for q in range(per_block)], axis=1)
+        line = matmul(bins.astype(BF16), taps_ref[b]).astype(BF16).astype(F32)
+        kr, ki = line[None, :lines], line[None, lines:]
+        tr = (kr * shift_r - ki * shift_i).astype(BF16)
+        ti = (kr * shift_i + ki * shift_r).astype(BF16)
+        lane = b * LANES
+        turned[:, 0:lines, lane:lane + LANES] = tr
+        turned[:, 0:lines, band + lane:band + lane + LANES] = -ti
+        turned[:, lines:2 * lines, lane:lane + LANES] = ti
+        turned[:, lines:2 * lines, band + lane:band + lane + LANES] = tr
+    table_copy.wait()
+    part = matmul_nt(turned[...].reshape(devices * 2 * lines, 2 * band), col_buf[...])
+    part_out[...] = part.astype(BF16).reshape(part_out.shape)
+
+    own_part = pltpu.make_async_copy(part_out.at[me], part_in.at[me], local_sem.at[1])
+    own_part.start()
+    part_copies = []
+    for r in range(1, devices):
+        other = (me + r) % devices
+        copy = pltpu.make_async_remote_copy(
+            part_out.at[other], part_in.at[me], part_send.at[r], part_recv.at[r],
+            device_id=whole_id(other), device_id_type=MESH)
+        copy.start()
+        part_copies.append(copy)
+    own_part.wait()
+    for copy in part_copies:
+        copy.wait()
+
+    per_sub = n_range * n_sub
+    out_rows = col_buf.shape[0]
+    for k in range(per_sub):
+        acc = part_in[k].astype(F32)
+        for d in range(1, n_pulse):
+            acc = acc + part_in[d * per_sub + k].astype(F32)
+        xx, ss = k // n_sub, k % n_sub
+        for c in range(2):
+            for d in range(n_pulse):
+                src = c * lines + d * pulses
+                dst = c * total + ((d * n_sub + ss) * n_range + xx) * pulses
+                sums[dst:dst + pulses, :] = acc[src:src + pulses]
+    real = jnp.transpose(sums[0:total, :])
+    imag = jnp.transpose(sums[total:2 * total, :])
+    lhs_ref[0:out_rows, :] = jnp.concatenate([real, -imag], axis=1).astype(BF16)
+    lhs_ref[out_rows:2 * out_rows, :] = jnp.concatenate([imag, real], axis=1).astype(BF16)
+
+
+def low_rank_body(raw_echo, range_taps, azim_taps, tile_col):
+    n_range, n_pulse, n_sub = lax.axis_size("range"), lax.axis_size("pulse"), lax.axis_size("sub")
+    devices = n_range * n_pulse * n_sub
+    shard_pulses, shard_samples = raw_echo.shape[1], raw_echo.shape[2]
+    samples = shard_samples * n_range
+    pulses = shard_pulses // n_range
+    blocks, block_bins, block_rows = range_taps.shape
+    grid = blocks * block_rows * n_pulse
+    width = azim_taps.shape[1]
+    tiles = grid // width
+    rows = grid // devices
+    upper = grid // LANES
+    half = upper // 2
+    total = shard_pulses * n_pulse * n_sub
+    lines = n_pulse * pulses
+    band_rows = samples // LANES // n_pulse
+
+    raw = raw_echo.reshape(2, shard_pulses, shard_samples // LANES, LANES)
+    az = azim_taps.reshape(shard_pulses, width // upper, 2, half).transpose(3, 0, 2, 1)
+    az = az.reshape(half, shard_pulses, LANES)
+    phase = (tile_col * jnp.arange(LANES, dtype=jnp.int32)[None, :] % tiles).astype(F32) * (2.0 * math.pi / tiles)
+    az = jnp.concatenate([az, jnp.stack([jnp.cos(phase), jnp.sin(phase)]).astype(BF16)])
+    az = az.reshape((half + 2) * shard_pulses, LANES)
+    left, right, twist = pulse_tables(samples, n_range)
+    coltab, shift = column_tables(grid, n_pulse, rows, devices)
+    rowtab = row_table(grid, width)
+
+    vmem = pl.BlockSpec(memory_space=pltpu.VMEM)
+    lhs, rhs = pl.pallas_call(
+        functools.partial(form_kernel, (n_pulse, n_range, n_sub)),
+        out_shape=(
+            jax.ShapeDtypeStruct((2 * rows, 2 * total), BF16),
+            jax.ShapeDtypeStruct((2 * total, grid), BF16),
+        ),
+        in_specs=[vmem] * 8 + [pl.BlockSpec(memory_space=pl.ANY)],
+        out_specs=(vmem, vmem),
+        scratch_shapes=[
+            pltpu.VMEM((n_range, 2, pulses, shard_samples // LANES, LANES), BF16),
+            pltpu.VMEM((n_pulse * n_sub,) + az.shape, BF16),
+            pltpu.VMEM((n_pulse, 2, pulses, band_rows, LANES), BF16),
+            pltpu.VMEM((n_pulse, 2, pulses, band_rows, LANES), BF16),
+            pltpu.VMEM((2 * lines * band_rows, LANES), F32),
+            pltpu.VMEM((half + 1, total, 4 * LANES), F32),
+            pltpu.VMEM((devices, 2 * lines, 2 * grid // n_pulse), BF16),
+            pltpu.VMEM((rows, 2 * grid // n_pulse), BF16),
+            pltpu.VMEM((devices, 2 * lines, rows), BF16),
+            pltpu.VMEM((devices, 2 * lines, rows), BF16),
+            pltpu.VMEM((2 * total, rows), F32),
+            pltpu.SemaphoreType.DMA((3,)),
+            pltpu.SemaphoreType.DMA((n_range,)),
+            pltpu.SemaphoreType.DMA((n_range,)),
+            pltpu.SemaphoreType.DMA((n_pulse * n_sub,)),
+            pltpu.SemaphoreType.DMA((n_pulse * n_sub,)),
+            pltpu.SemaphoreType.DMA((n_pulse,)),
+            pltpu.SemaphoreType.DMA((n_pulse,)),
+            pltpu.SemaphoreType.DMA((devices,)),
+            pltpu.SemaphoreType.DMA((devices,)),
+        ],
+        compiler_params=pltpu.CompilerParams(
+            collective_id=0, has_side_effects=True, vmem_limit_bytes=40 * 2 ** 20),
+    )(raw, az, left, right, twist, shift, range_taps, rowtab, coltab)
+    image = jnp.dot(lhs, rhs, preferred_element_type=F32)
+    return image.reshape(2, rows, grid)
+
+
+def body(raw_echo, range_taps, azim_taps, tile_col):
+    n_range, n_pulse, n_sub = lax.axis_size("range"), lax.axis_size("pulse"), lax.axis_size("sub")
+    samples = raw_echo.shape[2] * n_range
+    grid = range_taps.shape[0] * range_taps.shape[2] * n_pulse
+    pulses = raw_echo.shape[1] * n_pulse * n_sub
+    band_rows = samples // LANES // n_pulse
+    low_rank = 16 * pulses <= grid
+    fits = (
+        samples == LANES * LANES
+        and azim_taps.shape[1] * 2 * LANES == grid * LANES
+        and grid // LANES * LANES == grid
+        and azim_taps.shape[1] // (grid // LANES) * 2 == LANES
+        and range_taps.shape[2] == LANES
+        and band_rows % 16 == 0
+        and pulses % 16 == 0
+        and raw_echo.shape[1] == 8
+        and grid // (n_range * n_pulse * n_sub) % LANES == 0
+    )
+    if low_rank and fits:
+        return low_rank_body(raw_echo, range_taps, azim_taps, tile_col)
+    return general_body(raw_echo, range_taps, azim_taps, tile_col)
+
+
 def solution(mesh):
     placed = (
         P(None, ("groups", "pulse", "sub"), "range"),

time: 459 us -> 43.8 us (0.10); the launches traced: 452 us -> 43.4 us
  blocking collectives: 148 us -> 0 us
  waiting for transfers between devices: 105 us -> 0 us
  matrix products: 85.8 us -> 4.64 us
  local copies, waits for them, and re-layouts: 84.9 us -> 10.7 us
  Pallas kernels: 0 us -> 27.1 us
  starting transfers between devices: 21.2 us -> 0 us
  other arithmetic: 7.26 us -> 0.78 us
    all_to_all x2 -> x0, blocking collectives: 148 us -> none  [the longest x1 95.9 us: body(): lax.all_to_all(as_sent(columns_done), 'pulse', split_axis=2, concat_axis=...]
    all_to_all x4 -> x0, waiting for transfers between devices: 105 us -> none  [the longest x1 93.5 us: body(): lax.all_to_all(shaped.astype(jnp.bfloat16), 'pulse', split_axis=1, concat...]
    dot_general x29 -> x1, matrix products: 85.8 us -> 4.64 us  [low_rank_body(): image = jnp.dot(lhs, rhs, preferred_element_type=F32)]
    all_to_all x6 -> x0, local copies, waits for them, and re-layouts: 32.2 us -> none  [the longest x3 20.1 us: body(): lax.all_to_all(as_sent(columns_done), 'pulse', split_axis=2, concat_axis=...]
    convert_element_type x4 -> x0, local copies, waits for them, and re-layouts: 27.8 us -> none  [the longest x1 25.5 us: as_sent(): a.astype(jnp.bfloat16)]
    pallas_call x0 -> x1, Pallas kernels: none -> 27.1 us  [low_rank_body(): pl.pallas_call(functools.partial(form_kernel, (n_pulse, n_range, n_sub)),...]
    all_to_all x4 -> x0, starting transfers between devices: 21 us -> none  [the longest x1 6.31 us: body(): lax.all_to_all(flat_lines, ('pulse', 'range'), split_axis=0, concat_axis=...]
    another operation x7 -> x0, local copies, waits for them, and re-layouts: 9.49 us -> none  [the longest x1 8.98 us: body(): return jnp.stack([real_out, imag_out])]
  transfers between devices with their start and end apart: 6 -> 0, of which waited for: 3 -> 0; matrix products, arithmetic and copies ran while one was open for 3% -> 0% of each run, Pallas kernels for 0% -> 0%
where the time goes in v1:
time: 43.8 us; the launch traced here: 43.4 us
  Pallas kernels  27.1 us (62%)
  local copies, waits for them, and re-layouts  10.7 us (24%)
  matrix products  4.64 us (11%)
  other arithmetic  0.78 us (2%)
    pallas_call x1, Pallas kernels, low_rank_body(): pl.pallas_call(functools.partial(form_kernel, (n_pulse, n_range, n_sub)),...  27.1 us
    unnamed x15, local copies, waits for them, and re-layouts  9.51 us
    dot_general x1, matrix products, low_rank_body(): image = jnp.dot(lhs, rhs, preferred_element_type=F32)  4.64 us
    reshape x1, local copies, waits for them, and re-layouts, low_rank_body(): azim_taps.reshape(shard_pulses, width // upper, 2, half)  0.99 us

profile of v1, /device:TPU:0, one launch (start us, length us, event | category | flops | bytes accessed | tf_op | source)
XLA Modules:
  0.0 43.4 jit_solution(6902157709247831501)
XLA Ops:
  0.0 0.8 %cosine_convert_fusion = (bf16[1,8,128]{2,1,0:T(8,128)(2,1)S(1)}, bf16[1,8,128]{2,1,0:T(8,128)(2,1)S(1)}) fusion(s32[8]{0:T(128)} %bitcast.15), kind=kLoop, calls=%fused_computation.9 | loop fusion | flops 16384 | bytes 4128 | tf_op jit(solution)/shard_map/convert
  0.8 1.0 %copy.15 = bf16[2,8,64,128]{3,2,1,0:T(8,128)(2,1)S(1)} copy(bf16[2,8,64,128]{3,1,2,0:T(8,128)(2,1)} %bitcast.14) | data formatting | bytes 524288
  1.8 1.0 %reshape.131 = bf16[8,64,2,16]{3,2,1,0:T(2,128)(2,1)S(1)} reshape(bf16[8,2048]{1,0:T(8,128)(2,1)} %param.12) | data formatting | bytes 65536 | tf_op jit(solution)/shard_map/reshape | solution.py:442
  2.8 0.1 copy.12
  2.9 0.1 reshape.132
  3.0 0.0 copy-start
  3.1 2.2 %copy-done = bf16[4,256,2048]{2,1,0:T(8,128)(2,1)S(1)} copy-done((bf16[4,256,2048]{2,1,0:T(8,128)(2,1)S(1)}, bf16[4,256,2048]{2,1,0:T(8,128)(2,1)}, u32[]{:S(2)}) %copy-start) | copy-done | bytes 4194328
  5.2 0.0 copy-start.1
  5.2 1.6 %copy-done.1 = bf16[16,128,512]{2,1,0:T(8,128)(2,1)S(1)} copy-done((bf16[16,128,512]{2,1,0:T(8,128)(2,1)S(1)}, bf16[16,128,512]{2,1,0:T(8,128)(2,1)}, u32[]{:S(2)}) %copy-start.1) | copy-done | bytes 2097176
  6.8 0.0 copy-start.2
  6.8 1.2 %copy-done.2 = bf16[8,512,128]{2,1,0:T(8,128)(2,1)S(1)} copy-done((bf16[8,512,128]{2,1,0:T(8,128)(2,1)S(1)}, bf16[8,512,128]{2,1,0:T(8,128)(2,1)}, u32[]{:S(2)}) %copy-start.2) | copy-done | bytes 1048600
  8.1 0.0 copy-start.3
  8.1 0.9 %copy-done.3 = bf16[2,256,256]{2,1,0:T(8,128)(2,1)S(1)} copy-done((bf16[2,256,256]{2,1,0:T(8,128)(2,1)S(1)}, bf16[2,256,256]{2,1,0:T(8,128)(2,1)}, u32[]{:S(2)}) %copy-start.3) | copy-done | bytes 262168
  9.0 0.0 copy-start.4
  9.0 0.9 %copy-done.4 = bf16[2,256,256]{2,1,0:T(8,128)(2,1)S(1)} copy-done((bf16[2,256,256]{2,1,0:T(8,128)(2,1)S(1)}, bf16[2,256,256]{2,1,0:T(8,128)(2,1)}, u32[]{:S(2)}) %copy-start.4) | copy-done | bytes 262168
  10.0 0.0 copy-start.5
  10.0 0.9 %copy-done.5 = f32[2,128,128]{2,1,0:T(8,128)S(1)} copy-done((f32[2,128,128]{2,1,0:T(8,128)S(1)}, f32[2,128,128]{2,1,0:T(8,128)}, u32[]{:S(2)}) %copy-start.5) | copy-done | bytes 131096
  10.9 0.0 copy-start.6
  10.9 0.7 %copy-done.6 = f32[2,16,1,128]{3,2,1,0:T(1,128)S(1)} copy-done((f32[2,16,1,128]{3,2,1,0:T(1,128)S(1)}, f32[2,16,1,128]{3,2,1,0:T(1,128)}, u32[]{:S(2)}) %copy-start.6) | copy-done | bytes 16408
  11.6 27.1 %shard_map.100 = (bf16[512,128]{1,0:T(8,128)(2,1)S(1)}, bf16[128,4096]{1,0:T(8,128)(2,1)S(1)}) custom-call(bf16[2,8,64,128]{3,2,1,0:T(8,128)(2,1)S(1)} %copy.15, bf16[144,128]{1,0:T(8,128)(2,1)S(1)} %maximum_bitcast_fusion.az_ref, bf16[2,256,256]{2,1,0:T(8,128)(2,1)S(1)} %copy-done.4, bf16[2,256,256]{2,1,0:T(8,128)(2,1)S(1)} %copy-done.3, ...), custom_call_target="tpu_custom_call" | custom-call | tf_op jit(solution)/shard_map/pallas_call | solution.py:452
  38.7 4.6 %fusion.6 = f32[512,4096]{1,0:T(8,128)} fusion(bf16[512,128]{1,0:T(8,128)(2,1)S(1)} %get-tuple-element.7, bf16[128,4096]{1,0:T(8,128)(2,1)S(1)} %get-tuple-element.8), kind=kOutput, calls=%fused_computation.13 | convolution fusion | flops 536870912 | bytes 9568256 | tf_op jit(solution)/shard_map/dot_general | solution.py:485
  (1 shorter events, 0.0 us)
Async XLA Ops:
  3.0 2.2 %copy-start = (bf16[4,256,2048]{2,1,0:T(8,128)(2,1)S(1)}, bf16[4,256,2048]{2,1,0:T(8,128)(2,1)}, u32[]{:S(2)}) copy-start(bf16[4,256,2048]{2,1,0:T(8,128)(2,1)} %constant.34.clone.coltab_ref) | copy-start | bytes 12582916
  5.2 1.6 %copy-start.1 = (bf16[16,128,512]{2,1,0:T(8,128)(2,1)S(1)}, bf16[16,128,512]{2,1,0:T(8,128)(2,1)}, u32[]{:S(2)}) copy-start(bf16[16,128,512]{2,1,0:T(8,128)(2,1)} %constant.33.clone.rowtab_ref) | copy-start | bytes 6291460
  6.8 1.2 %copy-start.2 = (bf16[8,512,128]{2,1,0:T(8,128)(2,1)S(1)}, bf16[8,512,128]{2,1,0:T(8,128)(2,1)}, u32[]{:S(2)}) copy-start(bf16[8,512,128]{2,1,0:T(8,128)(2,1)} %taps_ref.1) | copy-start | bytes 3145732
  8.1 0.9 %copy-start.3 = (bf16[2,256,256]{2,1,0:T(8,128)(2,1)S(1)}, bf16[2,256,256]{2,1,0:T(8,128)(2,1)}, u32[]{:S(2)}) copy-start(bf16[2,256,256]{2,1,0:T(8,128)(2,1)} %constant.30.clone.right_ref) | copy-start | bytes 786436
  9.0 0.9 %copy-start.4 = (bf16[2,256,256]{2,1,0:T(8,128)(2,1)S(1)}, bf16[2,256,256]{2,1,0:T(8,128)(2,1)}, u32[]{:S(2)}) copy-start(bf16[2,256,256]{2,1,0:T(8,128)(2,1)} %constant.29.clone.left_ref) | copy-start | bytes 786436
  10.0 0.9 %copy-start.5 = (f32[2,128,128]{2,1,0:T(8,128)S(1)}, f32[2,128,128]{2,1,0:T(8,128)}, u32[]{:S(2)}) copy-start(f32[2,128,128]{2,1,0:T(8,128)} %constant.31.clone.twist_ref) | copy-start | bytes 393220
  10.9 0.7 %copy-start.6 = (f32[2,16,1,128]{3,2,1,0:T(1,128)S(1)}, f32[2,16,1,128]{3,2,1,0:T(1,128)}, u32[]{:S(2)}) copy-start(f32[2,16,1,128]{3,2,1,0:T(1,128)} %constant.32.clone.shift_ref) | copy-start | bytes 49156

commit v2 on v1

--- a/solution.py
+++ b/solution.py
@@ -247,10 +247,10 @@
 
 def form_kernel(
     sizes,
-    raw_ref, az_ref, left_ref, right_ref, twist_ref, shift_ref, taps_ref, rowtab_ref, coltab_ref,
+    raw_ref, az_ref, left_hbm, right_hbm, twist_hbm, shift_hbm, taps_hbm, rowtab_hbm, coltab_hbm,
     lhs_ref, rhs_ref,
-    x_buf, az_buf, sp_out, sp_in, sp_f32, planes, turned, col_buf, part_out, part_in, sums,
-    local_sem, x_send, x_recv, az_send, az_recv, sp_send, sp_recv, part_send, part_recv,
+    left_ref, right_ref, twist_ref, shift_ref, taps_ref, rowtab_ref, x_buf, az_buf, sp_out, sp_in, sp_f32, planes, turned, col_buf, part_out, part_in, sums,
+    table_sem, local_sem, x_send, x_recv, az_send, az_recv, sp_send, sp_recv, part_send, part_recv,
 ):
     n_pulse, n_range, n_sub = sizes
     devices = n_pulse * n_range * n_sub
@@ -259,15 +259,21 @@
     shards = n_pulse * n_sub
     shard = z * n_sub + s
     pulses = x_buf.shape[2]
-    blocks = taps_ref.shape[0]
+    blocks = taps_hbm.shape[0]
     band_rows = sp_in.shape[3]
 
     def whole_id(index):
         rest = index // n_sub
         return {"pulse": rest // n_range, "range": rest % n_range, "sub": index % n_sub}
 
-    table_copy = pltpu.make_async_copy(coltab_ref.at[z], col_buf, local_sem.at[0])
-    table_copy.start()
+    tables = [
+        pltpu.make_async_copy(source, target, table_sem.at[i])
+        for i, (source, target) in enumerate([
+            (left_hbm, left_ref), (twist_hbm, twist_ref), (right_hbm, right_ref), (rowtab_hbm, rowtab_ref),
+            (taps_hbm, taps_ref), (shift_hbm, shift_ref), (coltab_hbm.at[z], col_buf)])]
+    left_copy, twist_copy, right_copy, row_copy, taps_copy, shift_copy, table_copy = tables
+    for copy in tables:
+        copy.start()
     own_raw = pltpu.make_async_copy(raw_ref.at[:, pl.ds(x * pulses, pulses)], x_buf.at[x], local_sem.at[1])
     own_raw.start()
     own_az = pltpu.make_async_copy(az_ref, az_buf.at[shard], local_sem.at[2])
@@ -299,22 +305,29 @@
     for copy in raw_copies:
         copy.wait()
 
+    left_copy.wait()
+    twist_copy.wait()
+    right_copy.wait()
     twist_r, twist_i = twist_ref[0], twist_ref[1]
+    samples = jnp.concatenate(
+        [jnp.concatenate([x_buf[h, c, p] for h in range(n_range) for c in range(2)], axis=0)
+         for p in range(pulses)], axis=1)
+    mixed = matmul(left_ref[0], samples) + matmul(left_ref[1], samples)
+    both = []
     for p in range(pulses):
-        samples = jnp.concatenate(
-            [x_buf[h, c, p] for h in range(n_range) for c in range(2)], axis=0)
-        mixed = matmul(left_ref[0], samples) + matmul(left_ref[1], samples)
-        mr, mi = mixed[:LANES], mixed[LANES:]
-        both = jnp.concatenate([mr * twist_r - mi * twist_i, mr * twist_i + mi * twist_r], axis=1)
-        high = both.astype(BF16)
-        low = (both - high.astype(F32)).astype(BF16)
-        bins = (matmul_nt(right_ref[0], high) + matmul_nt(right_ref[1], high)
-                + matmul_nt(right_ref[0], low)).astype(BF16)
-        for c in range(2):
-            for d in range(n_pulse):
+        lanes = slice(p * LANES, (p + 1) * LANES)
+        mr, mi = mixed[:LANES, lanes], mixed[LANES:, lanes]
+        both.append(jnp.concatenate([mr * twist_r - mi * twist_i, mr * twist_i + mi * twist_r], axis=1))
+    both = jnp.concatenate(both, axis=0)
+    high = both.astype(BF16)
+    low = (both - high.astype(F32)).astype(BF16)
+    bins = (matmul_nt(right_ref[0], high) + matmul_nt(right_ref[1], high)
+            + matmul_nt(right_ref[0], low)).astype(BF16)
+    for c in range(2):
+        for d in range(n_pulse):
+            for p in range(pulses):
                 start = c * LANES + d * band_rows
-                sp_out[d, c, p] = bins[start:start + band_rows]
-
+                sp_out[d, c, p] = bins[start:start + band_rows, p * LANES:(p + 1) * LANES]
     own_bins = pltpu.make_async_copy(sp_out.at[z], sp_in.at[z], local_sem.at[1])
     own_bins.start()
     bin_copies = []
@@ -329,8 +342,10 @@
     own_az.wait()
     for copy in az_copies:
         copy.wait()
+    row_copy.wait()
     residues = rowtab_ref.shape[0]
     per_shard = az_ref.shape[0] // (residues + 2)
+    total = shards * per_shard
     everything = [az_buf[q].astype(F32) for q in range(shards)]
 
     def of_residue(f):
@@ -338,33 +353,15 @@
 
     for f in range(residues):
         planes[f] = matmul(of_residue(f).astype(BF16), rowtab_ref[f])
-    total = shards * per_shard
     planes[residues, :, 0:LANES] = of_residue(residues)
     planes[residues, :, LANES:2 * LANES] = of_residue(residues + 1)
-    step_rows = 16
-
-    def row_step(i, carry):
-        rows = pl.ds(pl.multiple_of(i * step_rows, step_rows), step_rows)
-        rows_i = pl.ds(pl.multiple_of(total + i * step_rows, step_rows), step_rows)
-        pr = planes[residues, rows, 0:LANES]
-        pi = planes[residues, rows, LANES:2 * LANES]
-        for parity in range(2):
-            at = 2 * parity * LANES
-            real = [planes[f, rows, at:at + LANES] for f in range(residues)]
-            imag = [planes[f, rows, at + LANES:at + 2 * LANES] for f in range(residues)]
-            real, imag = plane_transform(real, imag)
-            for k in range(residues):
-                lane = (2 * k + parity) * LANES
-                rhs_ref[rows, lane:lane + LANES] = (real[k] * pr - imag[k] * pi).astype(BF16)
-                rhs_ref[rows_i, lane:lane + LANES] = (real[k] * pi + imag[k] * pr).astype(BF16)
-        return carry
-
-    lax.fori_loop(0, total // step_rows, row_step, 0)
-
     own_bins.wait()
     for copy in bin_copies:
         copy.wait()
     lines = n_pulse * pulses
+    taps_copy.wait()
+    shift_copy.wait()
+    table_copy.wait()
     for d in range(n_pulse):
         for c in range(2):
             for p in range(pulses):
@@ -385,7 +382,6 @@
         turned[:, 0:lines, band + lane:band + lane + LANES] = -ti
         turned[:, lines:2 * lines, lane:lane + LANES] = ti
         turned[:, lines:2 * lines, band + lane:band + lane + LANES] = tr
-    table_copy.wait()
     part = matmul_nt(turned[...].reshape(devices * 2 * lines, 2 * band), col_buf[...])
     part_out[...] = part.astype(BF16).reshape(part_out.shape)
 
@@ -399,6 +395,26 @@
             device_id=whole_id(other), device_id_type=MESH)
         copy.start()
         part_copies.append(copy)
+    step_rows = 16
+
+    def row_step(i, carry):
+        rows = pl.ds(pl.multiple_of(i * step_rows, step_rows), step_rows)
+        rows_i = pl.ds(pl.multiple_of(total + i * step_rows, step_rows), step_rows)
+        pr = planes[residues, rows, 0:LANES]
+        pi = planes[residues, rows, LANES:2 * LANES]
+        for parity in range(2):
+            at = 2 * parity * LANES
+            real = [planes[f, rows, at:at + LANES] for f in range(residues)]
+            imag = [planes[f, rows, at + LANES:at + 2 * LANES] for f in range(residues)]
+            real, imag = plane_transform(real, imag)
+            for k in range(residues):
+                lane = (2 * k + parity) * LANES
+                rhs_ref[rows, lane:lane + LANES] = (real[k] * pr - imag[k] * pi).astype(BF16)
+                rhs_ref[rows_i, lane:lane + LANES] = (real[k] * pi + imag[k] * pr).astype(BF16)
+        return carry
+
+    lax.fori_loop(0, total // step_rows, row_step, 0)
+
     own_part.wait()
     for copy in part_copies:
         copy.wait()
@@ -441,8 +457,10 @@
     raw = raw_echo.reshape(2, shard_pulses, shard_samples // LANES, LANES)
     az = azim_taps.reshape(shard_pulses, width // upper, 2, half).transpose(3, 0, 2, 1)
     az = az.reshape(half, shard_pulses, LANES)
-    phase = (tile_col * jnp.arange(LANES, dtype=jnp.int32)[None, :] % tiles).astype(F32) * (2.0 * math.pi / tiles)
-    az = jnp.concatenate([az, jnp.stack([jnp.cos(phase), jnp.sin(phase)]).astype(BF16)])
+    offsets = turn(np.outer(np.arange(tiles), np.arange(LANES)) / tiles)
+    offsets = np.stack([offsets.real, offsets.imag]).astype(np.float32)
+    phase = sum(jnp.where(tile_col[None] == t, offsets[:, None, t], 0.0) for t in range(tiles))
+    az = jnp.concatenate([az, phase.astype(BF16)])
     az = az.reshape((half + 2) * shard_pulses, LANES)
     left, right, twist = pulse_tables(samples, n_range)
     coltab, shift = column_tables(grid, n_pulse, rows, devices)
@@ -455,9 +473,15 @@
             jax.ShapeDtypeStruct((2 * rows, 2 * total), BF16),
             jax.ShapeDtypeStruct((2 * total, grid), BF16),
         ),
-        in_specs=[vmem] * 8 + [pl.BlockSpec(memory_space=pl.ANY)],
+        in_specs=[vmem] * 2 + [pl.BlockSpec(memory_space=pltpu.HBM)] * 7,
         out_specs=(vmem, vmem),
         scratch_shapes=[
+            pltpu.VMEM(left.shape, BF16),
+            pltpu.VMEM(right.shape, BF16),
+            pltpu.VMEM(twist.shape, F32),
+            pltpu.VMEM(shift.shape, F32),
+            pltpu.VMEM(range_taps.shape, BF16),
+            pltpu.VMEM(rowtab.shape, BF16),
             pltpu.VMEM((n_range, 2, pulses, shard_samples // LANES, LANES), BF16),
             pltpu.VMEM((n_pulse * n_sub,) + az.shape, BF16),
             pltpu.VMEM((n_pulse, 2, pulses, band_rows, LANES), BF16),
@@ -469,6 +493,7 @@
             pltpu.VMEM((devices, 2 * lines, rows), BF16),
             pltpu.VMEM((devices, 2 * lines, rows), BF16),
             pltpu.VMEM((2 * total, rows), F32),
+            pltpu.SemaphoreType.DMA((7,)),
             pltpu.SemaphoreType.DMA((3,)),
             pltpu.SemaphoreType.DMA((n_range,)),
             pltpu.SemaphoreType.DMA((n_range,)),
@@ -480,7 +505,7 @@
             pltpu.SemaphoreType.DMA((devices,)),
         ],
         compiler_params=pltpu.CompilerParams(
-            collective_id=0, has_side_effects=True, vmem_limit_bytes=40 * 2 ** 20),
+            collective_id=0, has_side_effects=True, vmem_limit_bytes=60 * 2 ** 20),
     )(raw, az, left, right, twist, shift, range_taps, rowtab, coltab)
     image = jnp.dot(lhs, rhs, preferred_element_type=F32)
     return image.reshape(2, rows, grid)
@@ -495,7 +520,6 @@
     low_rank = 16 * pulses <= grid
     fits = (
         samples == LANES * LANES
-        and azim_taps.shape[1] * 2 * LANES == grid * LANES
         and grid // LANES * LANES == grid
         and azim_taps.shape[1] // (grid // LANES) * 2 == LANES
         and range_taps.shape[2] == LANES

time: 43.8 us -> 39.3 us (0.90)
  local copies, waits for them, and re-layouts: 10.7 us -> 2.93 us
  matrix products: 4.64 us -> 5.94 us
  other arithmetic: 0.78 us -> 2.05 us
  Pallas kernels: 27.1 us -> 28 us
    unnamed x15 -> x1, local copies, waits for them, and re-layouts: 9.51 us -> 1.7 us
    dot_general x1, matrix products: 4.64 us -> 5.94 us  [low_rank_body(): image = jnp.dot(lhs, rhs, preferred_element_type=F32)]
    pallas_call x1, Pallas kernels: 27.1 us -> 28 us  [low_rank_body(): pl.pallas_call(functools.partial(form_kernel, (n_pulse, n_range, n_sub)),...]
    another operation x1 -> x0, other arithmetic: 0.77 us -> none
    convert_element_type x0 -> x1, other arithmetic: none -> 0.77 us  [low_rank_body(): az = jnp.concatenate([az, phase.astype(BF16)])]
    eq x0 -> x1, other arithmetic: none -> 0.66 us  [low_rank_body(): tile_col[None] == t]
    reshape x1, other arithmetic: 0.01 us -> 0.63 us  [low_rank_body(): az = az.reshape((half + 2) * shard_pulses, LANES)]
where the time goes in v2:
time: 39.3 us; the launch traced here: 38.9 us
  Pallas kernels  28 us (71%)
  matrix products  5.94 us (15%)
  local copies, waits for them, and re-layouts  2.93 us (7%)
  other arithmetic  2.05 us (5%)
    pallas_call x1, Pallas kernels, low_rank_body(): pl.pallas_call(functools.partial(form_kernel, (n_pulse, n_range, n_sub)),...  28 us
    dot_general x1, matrix products, low_rank_body(): image = jnp.dot(lhs, rhs, preferred_element_type=F32)  5.94 us
    unnamed x1, local copies, waits for them, and re-layouts  1.7 us
    reshape x1, local copies, waits for them, and re-layouts, low_rank_body(): azim_taps.reshape(shard_pulses, width // upper, 2, half)  0.99 us

profile of v2, /device:TPU:0, one launch (start us, length us, event | category | flops | bytes accessed | tf_op | source)
XLA Modules:
  0.0 38.9 jit_solution(14359535183864942464)
XLA Ops:
  0.0 0.7 %compare_bitcast_fusion.1 = (pred[8]{0:T(512)(128)(4,1)S(1)}, pred[8]{0:T(512)(128)(4,1)S(1)}) fusion(s32[8,1]{0,1:T(1,128)} %param.15), kind=kLoop, calls=%fused_computation.4 | loop fusion | flops 16 | bytes 48 | tf_op jit(solution)/shard_map/eq | solution.py:462
  0.7 0.8 %add_convert_fusion = bf16[2,8,128]{2,1,0:T(8,128)(2,1)S(1)} fusion(f32[2,128]{1,0:T(2,128)} %constant.34, f32[2,128]{1,0:T(2,128)} %constant.33, pred[8]{0:T(512)(128)(4,1)S(1)} %get-tuple-element.10, pred[8]{0:T(512)(128)(4,1)S(1)} %get-tuple-element.9), kind=kLoop, calls=%fused_computation.2 | loop fusion | flops 8192 | bytes 6160 | tf_op jit(solution)/shard_map/convert_element_type | solution.py:463
  1.4 1.7 %copy.17 = bf16[2,8,64,128]{3,2,1,0:T(8,128)(2,1)} copy(bf16[2,8,64,128]{3,1,2,0:T(8,128)(2,1)} %bitcast.17) | data formatting | bytes 524288
  3.1 1.0 %reshape.34 = bf16[8,64,2,16]{3,2,1,0:T(2,128)(2,1)S(1)} reshape(bf16[8,2048]{1,0:T(8,128)(2,1)} %param.14) | data formatting | bytes 65536 | tf_op jit(solution)/shard_map/reshape | solution.py:458
  4.1 0.1 copy.14
  4.3 0.1 reshape.35
  4.4 0.6 %maximum_bitcast_fusion.az_ref = bf16[144,128]{1,0:T(8,128)(2,1)} fusion(bf16[2,8,128]{2,1,0:T(8,128)(2,1)S(1)} %add_convert_fusion, bf16[16,8,128]{2,1,0:T(8,128)(2,1)S(1)} %reshape.35), kind=kLoop, calls=%fused_computation.1 | loop fusion | flops 18432 | bytes 73728 | tf_op jit(solution)/shard_map/reshape | solution.py:464
  5.0 28.0 %shard_map.118 = (bf16[512,128]{1,0:T(8,128)(2,1)}, bf16[128,4096]{1,0:T(8,128)(2,1)}) custom-call(bf16[2,8,64,128]{3,2,1,0:T(8,128)(2,1)} %copy.17, bf16[144,128]{1,0:T(8,128)(2,1)} %maximum_bitcast_fusion.az_ref, bf16[2,256,256]{2,1,0:T(8,128)(2,1)} %constant.24.clone.left_hbm, bf16[2,256,256]{2,1,0:T(8,128)(2,1)} %constant.25.clone.right_hbm, ...), custom_call_target="tpu_custom_call" | custom-call | tf_op jit(solution)/shard_map/pallas_call | solution.py:470
  33.0 5.9 %fusion = f32[512,4096]{1,0:T(8,128)} fusion(bf16[512,128]{1,0:T(8,128)(2,1)} %get-tuple-element.7, bf16[128,4096]{1,0:T(8,128)(2,1)} %get-tuple-element.8), kind=kOutput, calls=%fused_computation.5 | convolution fusion | flops 536870912 | bytes 9568256 | tf_op jit(solution)/shard_map/dot_general | solution.py:510

commit v3 on v2

--- a/solution.py
+++ b/solution.py
@@ -199,18 +199,23 @@
     return table, np.stack([shift.real, shift.imag]).astype(np.float32)[:, :, None, :]
 
 
-def row_table(grid, width):
+def row_tables(grid):
     upper = grid // LANES
-    half = upper // 2
-    f = np.arange(half)[:, None, None, None, None]
-    e = np.arange(2)[None, :, None, None, None]
-    i1 = np.arange(width // upper)[None, None, :, None, None]
-    parity = np.arange(2)[None, None, None, :, None]
-    x1 = np.arange(LANES)[None, None, None, None, :]
-    taps = upper * i1 + half * e + f
-    angle = turn(taps * x1 / grid + (half * e + f) * parity / upper) / math.sqrt(grid)
-    both = np.stack([angle.real, angle.imag], axis=4)
-    return both.reshape(half, 2 * (width // upper), 4 * LANES).astype(ml_dtypes.bfloat16)
+    twist = turn(np.outer(np.arange(upper), np.arange(LANES)) / grid)
+    k = np.arange(LANES)
+    second = turn(np.outer(k, k) / LANES) / math.sqrt(grid)
+    factor = np.concatenate([second.real, second.imag], axis=1).astype(ml_dtypes.bfloat16)
+    return np.stack([twist.real, twist.imag], axis=1).astype(np.float32), factor
+
+
+def plus(a, b):
+    return b if a is None else a if b is None else a + b
+
+
+def minus(a, b):
+    if b is None:
+        return a
+    return -b if a is None else a - b
 
 
 def plane_transform(real, imag):
@@ -225,15 +230,17 @@
         if k == 0:
             tr, ti = a, b
         elif 4 * k == count:
-            tr, ti = -b, a
+            tr, ti = minus(None, b), a
         else:
             c = math.cos(2.0 * math.pi * k / count)
             s = math.sin(2.0 * math.pi * k / count)
-            tr, ti = a * c - b * s, a * s + b * c
-        low_r.append(even_r[k] + tr)
-        low_i.append(even_i[k] + ti)
-        high_r.append(even_r[k] - tr)
-        high_i.append(even_i[k] - ti)
+            tr, ti = a * c, a * s
+            if b is not None:
+                tr, ti = tr - b * s, ti + b * c
+        low_r.append(plus(even_r[k], tr))
+        low_i.append(plus(even_i[k], ti))
+        high_r.append(minus(even_r[k], tr))
+        high_i.append(minus(even_i[k], ti))
     return low_r + high_r, low_i + high_i
 
 
@@ -247,9 +254,9 @@
 
 def form_kernel(
     sizes,
-    raw_ref, az_ref, left_hbm, right_hbm, twist_hbm, shift_hbm, taps_hbm, rowtab_hbm, coltab_hbm,
+    raw_in, az_in, tile_ref, left_hbm, right_hbm, twist_hbm, shift_hbm, taps_hbm, phase_hbm, factor_hbm, coltab_hbm,
     lhs_ref, rhs_ref,
-    left_ref, right_ref, twist_ref, shift_ref, taps_ref, rowtab_ref, x_buf, az_buf, sp_out, sp_in, sp_f32, planes, turned, col_buf, part_out, part_in, sums,
+    left_ref, right_ref, twist_ref, shift_ref, taps_ref, phase_ref, factor_ref, raw_f32, raw_ref, x_buf, az_ref, az_buf, sp_out, sp_in, sp_f32, spun, rhs_f32, turned, col_buf, part_out, part_in, sums,
     table_sem, local_sem, x_send, x_recv, az_send, az_recv, sp_send, sp_recv, part_send, part_recv,
 ):
     n_pulse, n_range, n_sub = sizes
@@ -269,11 +276,23 @@
     tables = [
         pltpu.make_async_copy(source, target, table_sem.at[i])
         for i, (source, target) in enumerate([
-            (left_hbm, left_ref), (twist_hbm, twist_ref), (right_hbm, right_ref), (rowtab_hbm, rowtab_ref),
-            (taps_hbm, taps_ref), (shift_hbm, shift_ref), (coltab_hbm.at[z], col_buf)])]
-    left_copy, twist_copy, right_copy, row_copy, taps_copy, shift_copy, table_copy = tables
+            (left_hbm, left_ref), (twist_hbm, twist_ref), (right_hbm, right_ref), (phase_hbm, phase_ref),
+            (factor_hbm, factor_ref), (taps_hbm, taps_ref), (shift_hbm, shift_ref), (coltab_hbm.at[z], col_buf)])]
+    left_copy, twist_copy, right_copy, phase_copy, factor_copy, taps_copy, shift_copy, table_copy = tables
     for copy in tables:
         copy.start()
+    chunks = raw_ref.shape[2]
+    shard_pulses = raw_ref.shape[1]
+    for c in range(2):
+        for j in range(chunks):
+            rows = pl.ds(c * shard_pulses * chunks + j, shard_pulses, stride=chunks)
+            raw_f32[rows, :] = raw_in[c, :, j * LANES:(j + 1) * LANES].astype(F32)
+    raw_ref[...] = raw_f32[...].astype(BF16).reshape(raw_ref.shape)
+    half_width = az_in.shape[1] // 2
+    weights = az_in[...].astype(F32)
+    sign = jnp.broadcast_to(1.0 - 2.0 * tile_ref[...].astype(F32), (shard_pulses, LANES))
+    az_ref[:, 0:half_width] = jnp.concatenate([weights[:, :half_width], weights[:, half_width:]], axis=0).astype(BF16)
+    az_ref[:, half_width:half_width + LANES] = jnp.concatenate([sign, sign], axis=0).astype(BF16)
     own_raw = pltpu.make_async_copy(raw_ref.at[:, pl.ds(x * pulses, pulses)], x_buf.at[x], local_sem.at[1])
     own_raw.start()
     own_az = pltpu.make_async_copy(az_ref, az_buf.at[shard], local_sem.at[2])
@@ -342,24 +361,49 @@
     own_az.wait()
     for copy in az_copies:
         copy.wait()
-    row_copy.wait()
-    residues = rowtab_ref.shape[0]
-    per_shard = az_ref.shape[0] // (residues + 2)
-    total = shards * per_shard
-    everything = [az_buf[q].astype(F32) for q in range(shards)]
-
-    def of_residue(f):
-        return jnp.concatenate([a[f * per_shard:(f + 1) * per_shard] for a in everything], axis=0)
-
-    for f in range(residues):
-        planes[f] = matmul(of_residue(f).astype(BF16), rowtab_ref[f])
-    planes[residues, :, 0:LANES] = of_residue(residues)
-    planes[residues, :, LANES:2 * LANES] = of_residue(residues + 1)
+    phase_copy.wait()
+    upper = phase_ref.shape[0]
+    half = upper // 2
+    total = shards * shard_pulses
+
+    def row_step(i, carry):
+        pair = [az_buf[2 * i].astype(F32), az_buf[2 * i + 1].astype(F32)]
+
+        def piece(top, lane):
+            return jnp.concatenate(
+                [a[top * shard_pulses:(top + 1) * shard_pulses, lane:lane + LANES] for a in pair], axis=0)
+
+        taps = [piece(c * LANES // half_width, c * LANES % half_width) for c in range(half)]
+        signed = piece(0, half_width)
+        rows = pl.ds(pl.multiple_of(2 * shard_pulses * i, 2 * shard_pulses), 2 * shard_pulses)
+        rows_i = pl.ds(pl.multiple_of(total + 2 * shard_pulses * i, 2 * shard_pulses), 2 * shard_pulses)
+        for parity in range(2):
+            if parity == 0:
+                real, imag = taps, [None] * half
+            else:
+                real = [t * signed * math.cos(2.0 * math.pi * c / upper) for c, t in enumerate(taps)]
+                imag = [t * signed * math.sin(2.0 * math.pi * c / upper) for c, t in enumerate(taps)]
+            real, imag = plane_transform(real, imag)
+            for m in range(half):
+                low = 2 * m + parity
+                pr, pi = phase_ref[low, 0:1, :], phase_ref[low, 1:2, :]
+                qr, qi = real[m] * pr, real[m] * pi
+                if imag[m] is not None:
+                    qr, qi = qr - imag[m] * pi, qi + imag[m] * pr
+                qr, qi = qr.astype(BF16), qi.astype(BF16)
+                spun[low, rows, 0:LANES] = qr
+                spun[low, rows, LANES:2 * LANES] = -qi
+                spun[low, rows_i, 0:LANES] = qi
+                spun[low, rows_i, LANES:2 * LANES] = qr
+        return carry
+
+    lax.fori_loop(0, shards // 2, row_step, 0)
     own_bins.wait()
     for copy in bin_copies:
         copy.wait()
     lines = n_pulse * pulses
     taps_copy.wait()
+    factor_copy.wait()
     shift_copy.wait()
     table_copy.wait()
     for d in range(n_pulse):
@@ -395,26 +439,9 @@
             device_id=whole_id(other), device_id_type=MESH)
         copy.start()
         part_copies.append(copy)
-    step_rows = 16
-
-    def row_step(i, carry):
-        rows = pl.ds(pl.multiple_of(i * step_rows, step_rows), step_rows)
-        rows_i = pl.ds(pl.multiple_of(total + i * step_rows, step_rows), step_rows)
-        pr = planes[residues, rows, 0:LANES]
-        pi = planes[residues, rows, LANES:2 * LANES]
-        for parity in range(2):
-            at = 2 * parity * LANES
-            real = [planes[f, rows, at:at + LANES] for f in range(residues)]
-            imag = [planes[f, rows, at + LANES:at + 2 * LANES] for f in range(residues)]
-            real, imag = plane_transform(real, imag)
-            for k in range(residues):
-                lane = (2 * k + parity) * LANES
-                rhs_ref[rows, lane:lane + LANES] = (real[k] * pr - imag[k] * pi).astype(BF16)
-                rhs_ref[rows_i, lane:lane + LANES] = (real[k] * pi + imag[k] * pr).astype(BF16)
-        return carry
-
-    lax.fori_loop(0, total // step_rows, row_step, 0)
-
+    for low in range(upper):
+        rhs_f32[pl.ds(low, LANES, stride=upper), :] = matmul_nt(factor_ref[...], spun[low])
+    rhs_ref[...] = rhs_f32[...].astype(BF16)
     own_part.wait()
     for copy in part_copies:
         copy.wait()
@@ -437,6 +464,10 @@
     lhs_ref[out_rows:2 * out_rows, :] = jnp.concatenate([imag, real], axis=1).astype(BF16)
 
 
+def image_kernel(lhs_ref, rhs_ref, out_ref):
+    out_ref[...] = matmul_nt(lhs_ref[...], rhs_ref[...])
+
+
 def low_rank_body(raw_echo, range_taps, azim_taps, tile_col):
     n_range, n_pulse, n_sub = lax.axis_size("range"), lax.axis_size("pulse"), lax.axis_size("sub")
     devices = n_range * n_pulse * n_sub
@@ -446,34 +477,23 @@
     blocks, block_bins, block_rows = range_taps.shape
     grid = blocks * block_rows * n_pulse
     width = azim_taps.shape[1]
-    tiles = grid // width
     rows = grid // devices
-    upper = grid // LANES
-    half = upper // 2
     total = shard_pulses * n_pulse * n_sub
     lines = n_pulse * pulses
     band_rows = samples // LANES // n_pulse
 
-    raw = raw_echo.reshape(2, shard_pulses, shard_samples // LANES, LANES)
-    az = azim_taps.reshape(shard_pulses, width // upper, 2, half).transpose(3, 0, 2, 1)
-    az = az.reshape(half, shard_pulses, LANES)
-    offsets = turn(np.outer(np.arange(tiles), np.arange(LANES)) / tiles)
-    offsets = np.stack([offsets.real, offsets.imag]).astype(np.float32)
-    phase = sum(jnp.where(tile_col[None] == t, offsets[:, None, t], 0.0) for t in range(tiles))
-    az = jnp.concatenate([az, phase.astype(BF16)])
-    az = az.reshape((half + 2) * shard_pulses, LANES)
     left, right, twist = pulse_tables(samples, n_range)
     coltab, shift = column_tables(grid, n_pulse, rows, devices)
-    rowtab = row_table(grid, width)
+    phase, factor = row_tables(grid)
 
     vmem = pl.BlockSpec(memory_space=pltpu.VMEM)
     lhs, rhs = pl.pallas_call(
         functools.partial(form_kernel, (n_pulse, n_range, n_sub)),
         out_shape=(
             jax.ShapeDtypeStruct((2 * rows, 2 * total), BF16),
-            jax.ShapeDtypeStruct((2 * total, grid), BF16),
+            jax.ShapeDtypeStruct((grid, 2 * total), BF16),
         ),
-        in_specs=[vmem] * 2 + [pl.BlockSpec(memory_space=pltpu.HBM)] * 7,
+        in_specs=[vmem] * 3 + [pl.BlockSpec(memory_space=pltpu.HBM)] * 8,
         out_specs=(vmem, vmem),
         scratch_shapes=[
             pltpu.VMEM(left.shape, BF16),
@@ -481,19 +501,24 @@
             pltpu.VMEM(twist.shape, F32),
             pltpu.VMEM(shift.shape, F32),
             pltpu.VMEM(range_taps.shape, BF16),
-            pltpu.VMEM(rowtab.shape, BF16),
+            pltpu.VMEM(phase.shape, F32),
+            pltpu.VMEM(factor.shape, BF16),
+            pltpu.VMEM((raw_echo.size // LANES, LANES), F32),
+            pltpu.VMEM((2, shard_pulses, shard_samples // LANES, LANES), BF16),
             pltpu.VMEM((n_range, 2, pulses, shard_samples // LANES, LANES), BF16),
-            pltpu.VMEM((n_pulse * n_sub,) + az.shape, BF16),
+            pltpu.VMEM((2 * shard_pulses, width // 2 + LANES), BF16),
+            pltpu.VMEM((n_pulse * n_sub, 2 * shard_pulses, width // 2 + LANES), BF16),
             pltpu.VMEM((n_pulse, 2, pulses, band_rows, LANES), BF16),
             pltpu.VMEM((n_pulse, 2, pulses, band_rows, LANES), BF16),
             pltpu.VMEM((2 * lines * band_rows, LANES), F32),
-            pltpu.VMEM((half + 1, total, 4 * LANES), F32),
+            pltpu.VMEM((grid // LANES, 2 * total, 2 * LANES), BF16),
+            pltpu.VMEM((grid, 2 * total), F32),
             pltpu.VMEM((devices, 2 * lines, 2 * grid // n_pulse), BF16),
             pltpu.VMEM((rows, 2 * grid // n_pulse), BF16),
             pltpu.VMEM((devices, 2 * lines, rows), BF16),
             pltpu.VMEM((devices, 2 * lines, rows), BF16),
             pltpu.VMEM((2 * total, rows), F32),
-            pltpu.SemaphoreType.DMA((7,)),
+            pltpu.SemaphoreType.DMA((8,)),
             pltpu.SemaphoreType.DMA((3,)),
             pltpu.SemaphoreType.DMA((n_range,)),
             pltpu.SemaphoreType.DMA((n_range,)),
@@ -506,8 +531,19 @@
         ],
         compiler_params=pltpu.CompilerParams(
             collective_id=0, has_side_effects=True, vmem_limit_bytes=60 * 2 ** 20),
-    )(raw, az, left, right, twist, shift, range_taps, rowtab, coltab)
-    image = jnp.dot(lhs, rhs, preferred_element_type=F32)
+    )(raw_echo, azim_taps, tile_col, left, right, twist, shift, range_taps, phase, factor, coltab)
+    columns = min(grid, 4 * LANES)
+    image = pl.pallas_call(
+        image_kernel,
+        grid=(grid // columns,),
+        out_shape=jax.ShapeDtypeStruct((2 * rows, grid), F32),
+        in_specs=[
+            pl.BlockSpec((2 * rows, 2 * total), lambda i: (0, 0)),
+            pl.BlockSpec((columns, 2 * total), lambda i: (i, 0)),
+        ],
+        out_specs=pl.BlockSpec((2 * rows, columns), lambda i: (0, i)),
+        compiler_params=pltpu.CompilerParams(vmem_limit_bytes=60 * 2 ** 20),
+    )(lhs, rhs)
     return image.reshape(2, rows, grid)
 
 
@@ -521,7 +557,8 @@
     fits = (
         samples == LANES * LANES
         and grid // LANES * LANES == grid
-        and azim_taps.shape[1] // (grid // LANES) * 2 == LANES
+        and azim_taps.shape[1] * 2 == grid
+        and grid % (8 * LANES) == 0
         and range_taps.shape[2] == LANES
         and band_rows % 16 == 0
         and pulses % 16 == 0

time: 39.3 us -> 37.8 us (0.962)
  Pallas kernels: 28 us -> 36.1 us
  matrix products: 5.94 us -> 0 us
  other arithmetic: 2.05 us -> 0 us
  local copies, waits for them, and re-layouts: 2.93 us -> 1.32 us
    pallas_call x0 -> x1, Pallas kernels: none -> 7.31 us  [low_rank_body(): pl.pallas_call(image_kernel, grid=(grid // columns,), out_shape=jax.Shape...]
    dot_general x1 -> x0, matrix products: 5.94 us -> none  [low_rank_body(): image = jnp.dot(lhs, rhs, preferred_element_type=F32)]
    reshape x2 -> x0, local copies, waits for them, and re-layouts: 1.09 us -> none  [the longest x1 0.99 us: low_rank_body(): azim_taps.reshape(shard_pulses, width // upper, 2, half)]
    pallas_call x1, Pallas kernels: 28 us -> 28.8 us  [low_rank_body(): pl.pallas_call(functools.partial(form_kernel, (n_pulse, n_range, n_sub)),...]
    convert_element_type x1 -> x0, other arithmetic: 0.77 us -> none  [low_rank_body(): az = jnp.concatenate([az, phase.astype(BF16)])]
    eq x1 -> x0, other arithmetic: 0.66 us -> none  [low_rank_body(): tile_col[None] == t]
    reshape x1 -> x0, other arithmetic: 0.63 us -> none  [low_rank_body(): az = az.reshape((half + 2) * shard_pulses, LANES)]
where the time goes in v3:
time: 37.8 us; the launch traced here: 37.5 us
  Pallas kernels  36.1 us (96%)
  local copies, waits for them, and re-layouts  1.32 us (3%)
    pallas_call x1, Pallas kernels, low_rank_body(): pl.pallas_call(functools.partial(form_kernel, (n_pulse, n_range, n_sub)),...  28.8 us
    pallas_call x1, Pallas kernels, low_rank_body(): pl.pallas_call(image_kernel, grid=(grid // columns,), out_shape=jax.Shape...  7.31 us
    unnamed x1, local copies, waits for them, and re-layouts  1.32 us

profile of v3, /device:TPU:0, one launch (start us, length us, event | category | flops | bytes accessed | tf_op | source)
XLA Modules:
  0.0 37.5 jit_solution(16176781738381969137)
XLA Ops:
  0.0 1.3 %copy.12.tile_ref = s32[8,1]{1,0:T(8,128)} copy(s32[8,1]{0,1:T(1,128)} %param.14) | data formatting | bytes 64 | tf_op args[3]
  1.3 28.8 %shard_map.109 = (bf16[512,128]{1,0:T(8,128)(2,1)}, bf16[4096,128]{1,0:T(8,128)(2,1)}) custom-call(bf16[2,8,8192]{2,1,0:T(8,128)(2,1)} %raw_in.1, bf16[8,2048]{1,0:T(8,128)(2,1)} %az_in.1, s32[8,1]{1,0:T(8,128)} %copy.12.tile_ref, bf16[2,256,256]{2,1,0:T(8,128)(2,1)} %constant.14.clone.left_hbm, bf16[2,256,256]{2,1,0:T(8,128)(2,1)} %constant.15.clone.right_hbm, ...), custom_call_target="tpu_custom_call" | custom-call | tf_op jit(solution)/shard_map/pallas_call | solution.py:490
  30.2 7.3 %shard_map.110 = f32[512,4096]{1,0:T(8,128)} custom-call(bf16[512,128]{1,0:T(8,128)(2,1)} %get-tuple-element.7.lhs_ref, bf16[4096,128]{1,0:T(8,128)(2,1)} %get-tuple-element.8.rhs_ref), custom_call_target="tpu_custom_call" | custom-call | tf_op jit(solution)/shard_map/pallas_call | solution.py:536

commit v4 on v3

--- a/solution.py
+++ b/solution.py
@@ -264,7 +264,6 @@
     z, x, s = lax.axis_index("pulse"), lax.axis_index("range"), lax.axis_index("sub")
     me = (z * n_range + x) * n_sub + s
     shards = n_pulse * n_sub
-    shard = z * n_sub + s
     pulses = x_buf.shape[2]
     blocks = taps_hbm.shape[0]
     band_rows = sp_in.shape[3]
@@ -290,12 +289,16 @@
     raw_ref[...] = raw_f32[...].astype(BF16).reshape(raw_ref.shape)
     half_width = az_in.shape[1] // 2
     weights = az_in[...].astype(F32)
-    sign = jnp.broadcast_to(1.0 - 2.0 * tile_ref[...].astype(F32), (shard_pulses, LANES))
+    square = (shard_pulses, shard_pulses)
+    diagonal = lax.broadcasted_iota(jnp.int32, square, 0) == lax.broadcasted_iota(jnp.int32, square, 1)
+    tiles = jnp.broadcast_to(tile_ref[...].astype(F32), square)
+    tiles = jnp.sum(jnp.where(diagonal, tiles, 0.0), axis=1, keepdims=True)
+    sign = jnp.broadcast_to(1.0 - 2.0 * tiles, (shard_pulses, LANES))
     az_ref[:, 0:half_width] = jnp.concatenate([weights[:, :half_width], weights[:, half_width:]], axis=0).astype(BF16)
     az_ref[:, half_width:half_width + LANES] = jnp.concatenate([sign, sign], axis=0).astype(BF16)
     own_raw = pltpu.make_async_copy(raw_ref.at[:, pl.ds(x * pulses, pulses)], x_buf.at[x], local_sem.at[1])
     own_raw.start()
-    own_az = pltpu.make_async_copy(az_ref, az_buf.at[shard], local_sem.at[2])
+    own_az = pltpu.make_async_copy(az_ref, az_buf.at[s, z], local_sem.at[2])
     own_az.start()
 
     barrier = pltpu.get_barrier_semaphore()
@@ -312,11 +315,10 @@
         copy.start()
         raw_copies.append(copy)
     az_copies = []
-    for r in range(1, shards):
-        other = (shard + r) % shards
+    for r in range(1, n_pulse):
         copy = pltpu.make_async_remote_copy(
-            az_ref, az_buf.at[shard], az_send.at[r], az_recv.at[r],
-            device_id={"pulse": other // n_sub, "range": x, "sub": other % n_sub}, device_id_type=MESH)
+            az_ref, az_buf.at[s, z], az_send.at[r], az_recv.at[r],
+            device_id={"pulse": (z + r) % n_pulse, "range": x, "sub": s}, device_id_type=MESH)
         copy.start()
         az_copies.append(copy)
 
@@ -361,13 +363,18 @@
     own_az.wait()
     for copy in az_copies:
         copy.wait()
+    core_copy = pltpu.make_async_remote_copy(
+        az_buf.at[s], az_buf.at[s], az_send.at[0], az_recv.at[0],
+        device_id={"pulse": z, "range": x, "sub": 1 - s}, device_id_type=MESH)
+    core_copy.start()
+    core_copy.wait()
     phase_copy.wait()
     upper = phase_ref.shape[0]
     half = upper // 2
     total = shards * shard_pulses
 
     def row_step(i, carry):
-        pair = [az_buf[2 * i].astype(F32), az_buf[2 * i + 1].astype(F32)]
+        pair = [az_buf[0, i].astype(F32), az_buf[1, i].astype(F32)]
 
         def piece(top, lane):
             return jnp.concatenate(
@@ -465,7 +472,9 @@
 
 
 def image_kernel(lhs_ref, rhs_ref, out_ref):
-    out_ref[...] = matmul_nt(lhs_ref[...], rhs_ref[...])
+    for start in range(0, rhs_ref.shape[0], 4 * LANES):
+        columns = slice(start, start + 4 * LANES)
+        out_ref[:, columns] = matmul_nt(lhs_ref[...], rhs_ref[columns])
 
 
 def low_rank_body(raw_echo, range_taps, azim_taps, tile_col):
@@ -507,7 +516,7 @@
             pltpu.VMEM((2, shard_pulses, shard_samples // LANES, LANES), BF16),
             pltpu.VMEM((n_range, 2, pulses, shard_samples // LANES, LANES), BF16),
             pltpu.VMEM((2 * shard_pulses, width // 2 + LANES), BF16),
-            pltpu.VMEM((n_pulse * n_sub, 2 * shard_pulses, width // 2 + LANES), BF16),
+            pltpu.VMEM((n_sub, n_pulse, 2 * shard_pulses, width // 2 + LANES), BF16),
             pltpu.VMEM((n_pulse, 2, pulses, band_rows, LANES), BF16),
             pltpu.VMEM((n_pulse, 2, pulses, band_rows, LANES), BF16),
             pltpu.VMEM((2 * lines * band_rows, LANES), F32),
@@ -522,8 +531,8 @@
             pltpu.SemaphoreType.DMA((3,)),
             pltpu.SemaphoreType.DMA((n_range,)),
             pltpu.SemaphoreType.DMA((n_range,)),
-            pltpu.SemaphoreType.DMA((n_pulse * n_sub,)),
-            pltpu.SemaphoreType.DMA((n_pulse * n_sub,)),
+            pltpu.SemaphoreType.DMA((n_pulse,)),
+            pltpu.SemaphoreType.DMA((n_pulse,)),
             pltpu.SemaphoreType.DMA((n_pulse,)),
             pltpu.SemaphoreType.DMA((n_pulse,)),
             pltpu.SemaphoreType.DMA((devices,)),
@@ -531,17 +540,17 @@
         ],
         compiler_params=pltpu.CompilerParams(
             collective_id=0, has_side_effects=True, vmem_limit_bytes=60 * 2 ** 20),
-    )(raw_echo, azim_taps, tile_col, left, right, twist, shift, range_taps, phase, factor, coltab)
-    columns = min(grid, 4 * LANES)
+    )(raw_echo, azim_taps, tile_col.reshape(1, shard_pulses), left, right, twist, shift, range_taps, phase, factor, coltab)
+    step_rows = min(rows, LANES)
     image = pl.pallas_call(
         image_kernel,
-        grid=(grid // columns,),
+        grid=(2 * rows // step_rows,),
         out_shape=jax.ShapeDtypeStruct((2 * rows, grid), F32),
         in_specs=[
-            pl.BlockSpec((2 * rows, 2 * total), lambda i: (0, 0)),
-            pl.BlockSpec((columns, 2 * total), lambda i: (i, 0)),
+            pl.BlockSpec((step_rows, 2 * total), lambda i: (i, 0)),
+            pl.BlockSpec((grid, 2 * total), lambda i: (0, 0)),
         ],
-        out_specs=pl.BlockSpec((2 * rows, columns), lambda i: (0, i)),
+        out_specs=pl.BlockSpec((step_rows, grid), lambda i: (i, 0)),
         compiler_params=pltpu.CompilerParams(vmem_limit_bytes=60 * 2 ** 20),
     )(lhs, rhs)
     return image.reshape(2, rows, grid)
@@ -563,6 +572,7 @@
         and band_rows % 16 == 0
         and pulses % 16 == 0
         and raw_echo.shape[1] == 8
+        and n_sub == 2
         and grid // (n_range * n_pulse * n_sub) % LANES == 0
     )
     if low_rank and fits:

time: 37.8 us -> 33.7 us (0.89)
  Pallas kernels: 36.1 us -> 33.5 us
  local copies, waits for them, and re-layouts: 1.32 us -> 0 us
    pallas_call x1, Pallas kernels: 7.31 us -> 5.56 us  [low_rank_body(): pl.pallas_call(image_kernel, grid=(2 * rows // step_rows,), out_shape=jax...]
    unnamed x1 -> x0, local copies, waits for them, and re-layouts: 1.32 us -> none
    pallas_call x1, Pallas kernels: 28.8 us -> 27.9 us  [low_rank_body(): pl.pallas_call(functools.partial(form_kernel, (n_pulse, n_range, n_sub)),...]
where the time goes in v4:
time: 33.7 us; the launch traced here: 33.5 us
  Pallas kernels  33.5 us (99%)
    pallas_call x1, Pallas kernels, low_rank_body(): pl.pallas_call(functools.partial(form_kernel, (n_pulse, n_range, n_sub)),...  27.9 us
    pallas_call x1, Pallas kernels, low_rank_body(): pl.pallas_call(image_kernel, grid=(2 * rows // step_rows,), out_shape=jax...  5.56 us

profile of v4, /device:TPU:0, one launch (start us, length us, event | category | flops | bytes accessed | tf_op | source)
XLA Modules:
  0.0 33.5 jit_solution(3649085791350242999)
XLA Ops:
  0.0 27.9 %shard_map.109 = (bf16[512,128]{1,0:T(8,128)(2,1)}, bf16[4096,128]{1,0:T(8,128)(2,1)}) custom-call(bf16[2,8,8192]{2,1,0:T(8,128)(2,1)} %raw_in.1, bf16[8,2048]{1,0:T(8,128)(2,1)} %az_in.1, s32[1,8]{1,0:T(1,128)} %bitcast.2, bf16[2,256,256]{2,1,0:T(8,128)(2,1)} %constant.14.clone.left_hbm, bf16[2,256,256]{2,1,0:T(8,128)(2,1)} %constant.15.clone.right_hbm, ...), custom_call_target="tpu_custom_call" | custom-call | tf_op jit(solution)/shard_map/pallas_call | solution.py:499
  27.9 5.6 %shard_map.110 = f32[512,4096]{1,0:T(8,128)} custom-call(bf16[512,128]{1,0:T(8,128)(2,1)} %get-tuple-element.7.lhs_ref, bf16[4096,128]{1,0:T(8,128)(2,1)} %get-tuple-element.8.rhs_ref), custom_call_target="tpu_custom_call" | custom-call | tf_op jit(solution)/shard_map/pallas_call | solution.py:545
